TPU v7x, 128 devices: a whole 4x4x4 slice. The times are simulated.
128 devices in a mesh: dp: 64 (over z, y_lo, x, core), mp: 2 (over y_hi).
Axes of the slice: x: 4, y: 4 (y_hi: 2, y_lo: 2; y = y_hi * 2 + y_lo), z: 4, core: 2. Of those that a mesh axis runs over, the one named last changes fastest.
Arguments:
- img_emb: bfloat16 [16384, 1792], P('dp'), may hold values from -4 to 4
- txt_emb: bfloat16 [16384, 1792], P('dp'), may hold values from -4 to 4
- pair_ids: int32 [16384], P('dp'), may hold values from 0 to 16383, as said below
- log_scale: float32 [1], replicated, may hold values from 2.45 to 2.6
- bias: float32 [1], replicated, may hold values from -9.5 to -9
Outputs:
- grad_image: bfloat16 [16384, 1792], P(('dp', 'mp'))
- grad_text: bfloat16 [16384, 1792], P(('dp', 'mp'))
- loss: float32 [1], replicated
Inputs may be any that keep to these rules, and one draw needn't show every extreme that they name: `pair_ids`: rows with equal ids are positives of each other; every row is a positive of its own row.
All inputs are finite; a program needn't handle non-finite values.
Results may differ from a plain program's by a relative error of at most 0.0054.
Values may be sent and summed in bfloat16 or wider, within the bound.
No kernel may reach another device: no remote copies, remote signals or barrier semaphores. Data moves between devices by JAX's collectives and lax.ppermute only.
A program may use at most 192 MiB of HBM per device.

v0:
```python
import functools

import jax
import jax.numpy as jnp
from jax import lax
from jax.experimental import pallas as pl
from jax.experimental.pallas import tpu as pltpu
from jax.sharding import Mesh
from jax.sharding import PartitionSpec as P

EPS = 1e-06
E = 1792
EX = E + 128
ROWS = 256
HALF = ROWS // 2
STEP = 2 * ROWS
LOG2E = 1.4426950408889634
VMEM = 56 << 20
f32 = jnp.float32
bf16 = jnp.bfloat16
AXES = ("z", "yl", "x", "c", "yh")
SIZES = (4, 2, 4, 2, 2)
NT = (((1,), (1,)), ((), ()))
NN = (((1,), (0,)), ((), ()))
TN = (((0,), (0,)), ((), ()))


def dot(a, b, dims):
    return lax.dot_general(a, b, dims, preferred_element_type=f32)


def tags_of(ids):
    n = ROWS
    eye = lax.broadcasted_iota(jnp.int32, (n, n), 0) == lax.broadcasted_iota(jnp.int32, (n, n), 1)
    hi = jnp.sum(jnp.where(eye, (ids >> 7).astype(f32), 0.0), axis=1, keepdims=True)
    lo = jnp.sum(jnp.where(eye, (ids & 127).astype(f32), 0.0), axis=1, keepdims=True)
    lane = lax.broadcasted_iota(jnp.int32, (n, 128), 1)
    return jnp.where(lane == 0, hi, jnp.where(lane == 1, lo, 0.0)).astype(bf16)


def unit(rows):
    values = rows.astype(f32)
    return (values * lax.rsqrt(jnp.sum(values * values, axis=1, keepdims=True) + EPS)).astype(bf16)


def text_kernel(pos_ref, core_ref, txt_ref, ids_ref, own_ref, tags_ref):
    del core_ref
    tags_ref[...] = tags_of(ids_ref[...])
    rows = pl.ds(pl.multiple_of(pos_ref[0] * HALF, HALF), HALF)
    own_ref[:, :E] = unit(txt_ref[rows, :])
    own_ref[:, E:] = tags_ref[rows, :]


def image_kernel(scalars_ref, img_ref, tags_ref, *refs):
    del scalars_ref
    out_ref = refs[-1]
    out_ref[:, :E] = unit(img_ref[...])
    out_ref[:, E:] = tags_ref[...]


VM = pl.BlockSpec(memory_space=pltpu.VMEM)
SM = pl.BlockSpec(memory_space=pltpu.SMEM)


def kernel_call(body, ins, outs, scratch=(), ties=(), aliases={}, limit=6 << 20):
    specs = [SM if x.ndim == 1 else VM for x in ins] + [pl.BlockSpec(memory_space=pl.ANY)] * len(ties)
    return pl.pallas_call(
        body,
        in_specs=specs,
        out_specs=[VM] * len(outs),
        out_shape=[jax.ShapeDtypeStruct(*o) for o in outs],
        scratch_shapes=list(scratch),
        input_output_aliases=dict(aliases),
        compiler_params=pltpu.CompilerParams(vmem_limit_bytes=limit),
        cost_estimate=pl.CostEstimate(flops=0, bytes_accessed=0, transcendentals=0),
    )(*ins, *ties)


def id_row(tags):
    lane = lax.broadcasted_iota(jnp.int32, (8, 128), 1)
    pick = jnp.where(lane == 0, 128.0, jnp.where(lane == 1, 1.0, 0.0)).astype(bf16)
    return dot(pick, tags, NT)


def id_col(tags):
    parts = tags[:, :2].astype(f32)
    return parts[:, 0:1] * 128.0 + parts[:, 1:2]


def pair_terms(products, same, temper, scale, shift):
    t = products * scale + shift
    e = jnp.exp2(jnp.where(same, -t, t))
    u = 1.0 + e
    r = pltpu.reciprocal(u, approx=True)
    r = r * (2.0 - u * r)
    coef = (jnp.where(same, -temper, temper) * (e * r)).astype(bf16)
    loss = jnp.log(u) + (e - (u - 1.0)) * r
    return coef, loss


def logits_kernel(n_i, n_t, old_i, old_t, *refs):
    refs = list(refs)
    sc = refs.pop(0)
    new_i, new_t = refs[:n_i], refs[n_i : n_i + n_t]
    refs = refs[n_i + n_t :]
    had_i, had_t = refs[:old_i], refs[old_i : old_i + old_t]
    outs, (coef_ref, loss_ref, trow, i_sem, t_sem) = refs[old_i + old_t : -5], refs[-5:]
    temper, scale, shift = sc[0], sc[1], sc[2]
    rows = outs[0] if new_i else had_i[0]
    for k, ref in enumerate(new_i):
        pltpu.make_async_copy(ref, rows.at[pl.ds(k * ROWS, ROWS)], i_sem.at[k]).start()
    cols, copies = [], []
    for k, ref in enumerate(new_t):
        copy = pltpu.make_async_copy(ref, outs[-1].at[pl.ds(k * ROWS, ROWS)], t_sem.at[k])
        copy.start()
        cols.append(ref)
        copies.append(copy)
    for ref in had_t:
        cols += [ref.at[pl.ds(k, ROWS)] for k in range(0, ref.shape[0], ROWS)]
    loss_ref[...] = jnp.zeros_like(loss_ref)
    for j, text in enumerate(cols):
        trow[j] = id_row(text[:, E:])

    def step(image, here):
        column = id_col(image[:, E:])
        for j, text in enumerate(cols):
            products = dot(image[:, :E], text[:, :E], NT)
            coef, loss = pair_terms(products, column == trow[j, 0:1], temper, scale, shift)
            coef_ref[here, j * ROWS : (j + 1) * ROWS] = coef
            loss_ref[...] += jnp.sum(loss.reshape(image.shape[0] // 8, 8, ROWS), axis=0)

    def copied_step(k, carry):
        here = pl.ds(pl.multiple_of(k * STEP, STEP), STEP)
        for part in range(STEP // ROWS):
            piece = rows.at[pl.ds(pl.multiple_of(k * STEP + part * ROWS, ROWS), ROWS)]
            pltpu.make_async_copy(piece, piece, i_sem.at[k * (STEP // ROWS) + part]).wait()
        step(rows.at[here], here)
        return carry

    if n_i > 2:
        lax.fori_loop(0, n_i * ROWS // STEP, copied_step, 0)
    elif n_i:
        for k, ref in enumerate(new_i):
            step(ref, pl.ds(k * ROWS, ROWS))
        for k in range(n_i):
            piece = rows.at[pl.ds(k * ROWS, ROWS)]
            pltpu.make_async_copy(piece, piece, i_sem.at[k]).wait()
    else:
        for k in range(0, rows.shape[0], STEP):
            step(rows.at[pl.ds(k, STEP)], pl.ds(k, STEP))
    for copy in copies:
        copy.wait()


def logits(scalars, new_i=(), new_t=(), old_i=(), old_t=()):
    total = [sum(x.shape[0] for x in group) for group in (new_i, new_t, old_i, old_t)]
    rows, cols = total[0] + total[2], total[1] + total[3]
    return kernel_call(
        functools.partial(logits_kernel, len(new_i), len(new_t), len(old_i), len(old_t)),
        (scalars, *new_i, *new_t, *old_i, *old_t),
        [((n, EX), bf16) for n in total[:2] if n] + [((rows, cols), bf16), ((8, ROWS), f32)],
        scratch=[pltpu.VMEM((cols // ROWS, 8, ROWS), f32), pltpu.SemaphoreType.DMA((len(new_i) or 1,)), pltpu.SemaphoreType.DMA((len(new_t) or 1,))],
        limit=12 << 20,
    )


def block(core_ref, k):
    start = jnp.where(core_ref[0] == 0, k[0], k[1]) if isinstance(k, tuple) else k
    return pl.ds(pl.multiple_of(start * ROWS, ROWS), ROWS)


def image_grads_kernel(blocks, parts, losses, ties, core_ref, *refs):
    coefs, texts = refs[:parts], refs[parts : 2 * parts]
    losses, outs = refs[2 * parts : 2 * parts + losses], refs[2 * parts + losses + ties :]
    for out_ref, k in zip(outs, blocks):
        rows = block(core_ref, k)
        at, grad = 0, None
        for n, text in enumerate(texts):
            coef = coefs[n][rows, :] if coefs[n].shape[1] == text.shape[0] else coefs[n][rows, at : at + text.shape[0]]
            part = dot(coef, text[:, :E], NN)
            grad = part if grad is None else grad + part
            at += text.shape[0]
        out_ref[:ROWS, :] = grad.astype(bf16)
    if losses:
        put(outs[0], jnp.sum(sum(r[...] for r in losses)))


def text_grads_kernel(blocks, parts, ties, core_ref, *refs):
    coefs, images = refs[:parts], refs[parts : 2 * parts]
    for out_ref, ks in zip(refs[2 * parts + ties :], blocks):
        sums = [dot(c[:, block(core_ref, k)], i[:, :E], TN) for c, i, k in zip(coefs, images, ks)]
        out_ref[...] = sum(sums[1:], sums[0]).astype(bf16)


def image_grads(core, blocks, coefs, texts, losses=(), ties=()):
    first = ((ROWS + 16 if losses else ROWS, E), bf16)
    return kernel_call(
        functools.partial(image_grads_kernel, blocks, len(texts), len(losses), len(ties)),
        (core, *coefs, *texts, *losses),
        [first] + [((ROWS, E), bf16)] * (len(blocks) - 1),
        ties=ties,
        limit=10 << 20,
    )


def text_grads(core, blocks, coefs, images, ties=()):
    return kernel_call(
        functools.partial(text_grads_kernel, blocks, len(images), len(ties)),
        (core, *coefs, *images),
        [((ROWS, E), bf16)] * len(blocks),
        ties=ties,
        limit=10 << 20,
    )


def sum_kernel(*refs):
    refs[-1][...] = sum(r[...] for r in refs[:-1])


def sum_of(*parts):
    return kernel_call(sum_kernel, parts, [(parts[0].shape, parts[0].dtype)])[0]


def far_kernel(own_ref, got_ref, *refs):
    losses, (out_ref, loss_ref) = refs[:3], refs[-2:]
    out_ref[...] = (own_ref[...].astype(f32) + got_ref[:ROWS, :].astype(f32)).astype(bf16)
    loss_ref[...] = jnp.full((8, 128), jnp.sum(sum(r[...] for r in losses)) + take(got_ref), f32)


def stack_kernel(at_ref, a_ref, b_ref, *refs):
    n = a_ref.shape[0]
    out_ref = refs[-1]
    out_ref[pl.ds(pl.multiple_of(at_ref[0] * n, n), n), :] = a_ref[...]
    out_ref[pl.ds(pl.multiple_of((1 - at_ref[0]) * n, n), n), :] = b_ref[...]


def stacked(at, a, b, ties=()):
    return kernel_call(stack_kernel, (at, a, b), [((2 * a.shape[0], a.shape[1]), bf16)], ties=ties)[0]


def copy_kernel(in_ref, *refs):
    refs[-1][...] = in_ref[...]


def after(value, *ties):
    return kernel_call(copy_kernel, (value,), [(value.shape, value.dtype)], ties=ties)[0]


def put(ref, number):
    lane = lax.broadcasted_iota(jnp.int32, (16, 128), 1)
    rest = jnp.full((16, 128), number, f32)
    parts = []
    for _ in range(3):
        parts.append(rest.astype(bf16).astype(f32))
        rest = rest - parts[-1]
    value = jnp.where(lane == 0, parts[0], jnp.where(lane == 1, parts[1], jnp.where(lane == 2, parts[2], 0.0)))
    ref[ROWS:, :128] = value.astype(bf16)
    ref[ROWS:, 128:] = jnp.zeros((16, E - 128), bf16)


def take(ref):
    lane = lax.broadcasted_iota(jnp.int32, (16, 128), 1)
    row = lax.broadcasted_iota(jnp.int32, (16, 128), 0)
    return jnp.sum(jnp.where((lane < 3) & (row == 0), ref[ROWS:, :128].astype(f32), 0.0))


def gather_gate(core, t_low, t_high, i_low, i_high, t_out, i_out):
    for k, (text, image) in enumerate(((t_low, i_low), (t_high, i_high))):

        @pl.when(core[0] == k)
        def _():
            t_out[...], i_out[...] = text[...], image[...]


def near_kernel(parts, *refs):
    refs[-1][...] = sum(r[...].astype(f32) for r in refs[:parts]).astype(bf16)


def near(parts, ties=()):
    return kernel_call(functools.partial(near_kernel, len(parts)), parts, [((ROWS, E), bf16)], ties=ties)[0]


def text_split_kernel(*refs):
    keep_ref, send_ref = refs[-2:]
    keep_ref[...] = sum(r[:HALF, :].astype(f32) for r in refs[:3])
    send_ref[...] = sum(r[HALF:, :].astype(f32) for r in refs[:3]).astype(bf16)


def image_split_kernel(half, *refs):
    keep_ref, send_ref = refs[-2:]
    for which, out_ref in ((half[0], keep_ref), (1 - half[0], send_ref)):
        rows = pl.ds(pl.multiple_of(which * HALF, HALF), HALF)
        out_ref[...] = sum(r[rows, :].astype(f32) for r in refs[:4]).astype(out_ref.dtype)


def backward(raw, grad):
    values = raw.astype(f32)
    inverse = lax.rsqrt(jnp.sum(values * values, axis=1, keepdims=True) + EPS)
    unit_values = values * inverse
    inner = jnp.sum(unit_values * grad, axis=1, keepdims=True)
    return ((grad - unit_values * inner) * inverse).astype(bf16)


def last_kernel(pos_ref, img_ref, txt_ref, i_ref, ir_ref, *refs):
    t_refs, (gi_ref, gt_ref) = refs[:2], refs[2:]
    rows = pl.ds(pl.multiple_of(pos_ref[0] * HALF, HALF), HALF)
    gi_ref[...] = backward(img_ref[rows, :], i_ref[...] + ir_ref[...].astype(f32))
    gt_ref[...] = backward(txt_ref[rows, :], sum(r[...].astype(f32) for r in t_refs))


def ring(axis, by):
    n = SIZES[AXES.index(axis)]
    return [(i, (i + by) % n) for i in range(n)]


def both_ways(value, axis):
    return lax.ppermute(value, axis, ring(axis, 1)), lax.ppermute(value, axis, ring(axis, -1))


def by_core(value, axis, by=1):
    n = SIZES[AXES.index(axis)]
    perm = [(i * 2 + c, (i + (1 - 2 * c) * by) % n * 2 + c) for i in range(n) for c in range(2)]
    return lax.ppermute(value, (axis, "c"), perm)


def swapped(value, axis, bit=1):
    n = SIZES[AXES.index(axis)]
    return lax.ppermute(value, axis, [(i, i ^ bit) for i in range(n)])


def cross_y(value):
    perm = []
    for yl in range(2):
        for c in range(2):
            for yh in range(2):
                perm.append(((yl * 2 + c) * 2 + yh, ((1 - yl) * 2 + c) * 2 + (yh ^ c)))
    return lax.ppermute(value, ("yl", "c", "yh"), perm)


def local(img_emb, txt_emb, pair_ids, log_scale, bias):
    yh, c = lax.axis_index("yh"), lax.axis_index("c")
    core = c.reshape(1).astype(jnp.int32)
    zero = jnp.zeros((1,), jnp.int32)
    pos = yh.reshape(1).astype(jnp.int32)
    temper = jnp.exp(log_scale[0])
    scalars = jnp.stack([temper, temper * LOG2E, bias[0] * LOG2E])
    t_own, tags = kernel_call(
        text_kernel, (pos, core, txt_emb, pair_ids.reshape(1, ROWS)), [((HALF, EX), bf16), ((ROWS, 128), bf16)]
    )
    t_yl = cross_y(t_own)
    (i_own,) = kernel_call(image_kernel, (scalars, img_emb, tags), [((ROWS, EX), bf16)])
    i_own = after(i_own, t_yl)
    i_low, i_high = both_ways(i_own, "z")
    i_own_s = swapped(i_own, "c")
    t_own = stacked(zero, t_own, t_yl)
    t_low, t_high = both_ways(t_own, "x")
    t_pass, i_pass = kernel_call(
        gather_gate, (core, t_low, t_high, i_low, i_high), [((ROWS, EX), bf16)] * 2
    )
    t_far, i_far = by_core(t_pass, "x"), by_core(i_pass, "z")
    i_low_s, i_high_s = swapped(i_low, "c"), swapped(i_high, "c")
    i_near, t_near, p_near, loss_a = logits(
        scalars, (i_own, i_own_s, i_low, i_low_s, i_high, i_high_s), (t_own, t_low, t_high)
    )
    i_far = after(i_far, loss_a, t_far)
    i_far_s = swapped(i_far, "c")
    t_far, p_cols, loss_b = logits(scalars, (), (t_far,), (i_near,))
    i_far, p_rows, loss_c = logits(scalars, (i_far, i_far_s), (), (), (t_near, t_far))
    losses, texts, images = (loss_a, loss_b, loss_c), (t_near, t_far), (i_near, i_far)
    far_s, far = image_grads(core, (1, 0), (p_rows, p_rows), texts, losses)
    (t_far,) = text_grads(core, ((0, 3),), (p_cols, p_rows), images, ties=(far,))
    t_got = by_core(t_far, "x")
    z_far, loss = kernel_call(
        far_kernel, (far, swapped(far_s, "c"), *losses), [((ROWS, E), bf16), ((8, 128), f32)], ties=(t_far,)
    )
    z_got = by_core(z_far, "z")
    near_parts, near_texts = (p_near, p_cols), (p_near, p_rows)
    two_s, one = image_grads(core, ((5, 3), (2, 4)), near_parts, texts, ties=(z_far,))
    (t_one,) = text_grads(core, (((1, 2), (1, 2)),), near_texts, images, ties=(one,))
    t_from_one = by_core(t_one, "x", -1)
    z_one = near((one, swapped(two_s, "c")), ties=(t_one,))
    z_from_one = by_core(z_one, "z", -1)
    one_s, two = image_grads(core, ((3, 5), (4, 2)), near_parts, texts, ties=(z_one,))
    (t_two,) = text_grads(core, (((2, 1), (2, 1)),), near_texts, images, ties=(two,))
    own_s, own = image_grads(core, (1, 0), near_parts, texts, ties=(t_two,))
    (t_own,) = text_grads(core, ((0, 0),), near_texts, images, ties=(own,))
    got_two, got_own = swapped(one_s, "c"), swapped(own_s, "c")
    t_two = near((t_two, t_got), ties=(z_got, z_from_one, t_from_one, t_own))
    z_two = near((two, got_two, z_got), ties=(t_got, z_from_one, t_from_one, t_own, got_own))
    t_from_two, z_from_two = by_core(t_two, "x"), by_core(z_two, "z")
    loss = after(loss, z_two, t_two)
    flips = [[(i, i ^ bits) for i in range(4)] for bits in (1, 2, 3)]
    loss = sum_of(loss, *[lax.ppermute(loss, ("yl", "yh"), perm) for perm in flips])
    half = (HALF, E)
    t_keep, t_send = kernel_call(
        text_split_kernel, (t_own, t_from_one, t_from_two), [(half, f32), (half, bf16)], ties=(loss,)
    )
    i_keep, i_send = kernel_call(
        image_split_kernel, (pos, own, got_own, z_from_one, z_from_two), [(half, f32), (half, bf16)], ties=(t_send,)
    )
    loss = after(loss, i_send)
    i_recv = swapped(i_send, "yh")
    t_recv = cross_y(t_send)
    for axis in ("x", "z"):
        loss = sum_of(loss, *[lax.ppermute(loss, axis, ring(axis, by)) for by in (1, -1, 2)])
    grad_image, grad_text = kernel_call(
        last_kernel, (pos, img_emb, txt_emb, i_keep, i_recv, t_keep, t_recv), [((HALF, E), bf16)] * 2
    )
    return (grad_image, grad_text, loss[0, :1] / (64 * ROWS))


def solution(mesh):
    fine = Mesh(mesh.devices.reshape(SIZES), AXES)
    group = ("z", "yl", "x", "c")
    return jax.shard_map(
        local,
        mesh=fine,
        in_specs=(P(group, None), P(group, None), P(group), P(), P()),
        out_specs=(P(AXES, None), P(AXES, None), P()),
        check_vma=False,
    )
```

profile of v0, /device:TPU:0, one launch (start us, length us, event | category | flops | bytes accessed | tf_op | source)
XLA Modules:
  0.0 138.9 jit_solution(6497507967404185069)
XLA Ops:
  0.6 1.2 copy-done.2
  1.8 0.7 copy-done.4
  2.5 0.2 shard_map.76
  2.7 1.7 %collective-permute-start = (bf16[128,1920]{1,0:T(8,128)(2,1)S(1)}, bf16[128,1920]{1,0:T(8,128)(2,1)S(1)}, u32[]{:S(2)}, u32[]{:S(2)}) collective-permute-start(bf16[128,1920]{1,0:T(8,128)(2,1)S(1)} %get-tuple-element.34.a_ref), channel_id=1, source_target_pairs={{0,16},{1,17},{2,19},{3,18},{16,0},{17,1},{18,3},{19,2},{4,20},{5,... | collective-permute-start | bytes 1474568 | tf_op jit(solution)/shard_map/ppermute | solution.py:337
  5.9 1.2 copy-done
  7.1 0.8 shard_map.77.in_ref
  7.9 3.7 %collective-permute-done.refs_0_.b_ref = bf16[128,1920]{1,0:T(8,128)(2,1)S(1)} collective-permute-done((bf16[128,1920]{1,0:T(8,128)(2,1)S(1)}, bf16[128,1920]{1,0:T(8,128)(2,1)S(1)}, u32[]{:S(2)}, u32[]{:S(2)}) %collective-permute-start) | collective-permute-done | bytes 491552 | tf_op jit(solution)/shard_map/ppermute | solution.py:337
  11.7 4.2 %collective-permute-start.4 = (bf16[256,1920]{1,0:T(8,128)(2,1)S(1)}, bf16[256,1920]{1,0:T(8,128)(2,1)S(1)}, u32[]{:S(2)}, u32[]{:S(2)}) collective-permute-start(bf16[256,1920]{1,0:T(8,128)(2,1)S(1)} %shard_map.78.refs_1_), channel_id=1, source_target_pairs={{0,96},{32,0},{64,32},{96,64},{1,97},{33,1},{65,33},{97,65},{2,98}... | collective-permute-start | bytes 2949128 | tf_op jit(solution)/shard_map/ppermute | solution.py:317
  16.0 2.8 %collective-permute-start.7 = (bf16[256,1920]{1,0:T(8,128)(2,1)S(1)}, bf16[256,1920]{1,0:T(8,128)(2,1)S(1)}, u32[]{:S(2)}, u32[]{:S(2)}) collective-permute-start(bf16[256,1920]{1,0:T(8,128)(2,1)S(1)} %shard_map.79.refs_7_), channel_id=1, source_target_pairs={{0,12},{4,0},{8,4},{12,8},{1,13},{5,1},{9,5},{13,9},{2,14},{6,2},{... | collective-permute-start | bytes 2949128 | tf_op jit(solution)/shard_map/ppermute | solution.py:317
  18.8 18.2 %collective-permute-done.4.refs_5_.i_high = bf16[256,1920]{1,0:T(8,128)(2,1)S(1)} collective-permute-done((bf16[256,1920]{1,0:T(8,128)(2,1)S(1)}, bf16[256,1920]{1,0:T(8,128)(2,1)S(1)}, u32[]{:S(2)}, u32[]{:S(2)}) %collective-permute-start.4) | collective-permute-done | bytes 983072 | tf_op jit(solution)/shard_map/ppermute | solution.py:317
  37.0 3.4 %collective-permute-done.2.refs_3_.i_low = bf16[256,1920]{1,0:T(8,128)(2,1)S(1)} collective-permute-done((bf16[256,1920]{1,0:T(8,128)(2,1)S(1)}, bf16[256,1920]{1,0:T(8,128)(2,1)S(1)}, u32[]{:S(2)}, u32[]{:S(2)}) %collective-permute-start.2) | collective-permute-done | bytes 983072 | tf_op jit(solution)/shard_map/ppermute | solution.py:317
  40.5 2.6 %collective-permute-done.6.refs_8_.t_low = bf16[256,1920]{1,0:T(8,128)(2,1)S(1)} collective-permute-done((bf16[256,1920]{1,0:T(8,128)(2,1)S(1)}, bf16[256,1920]{1,0:T(8,128)(2,1)S(1)}, u32[]{:S(2)}, u32[]{:S(2)}) %collective-permute-start.6) | collective-permute-done | bytes 983072 | tf_op jit(solution)/shard_map/ppermute | solution.py:317
  43.1 0.1 shard_map.81
  43.4 10.9 %shard_map.80 = (bf16[1536,1920]{1,0:T(8,128)(2,1)S(1)}, bf16[768,1920]{1,0:T(8,128)(2,1)S(1)}, bf16[1536,768]{1,0:T(8,128)(2,1)S(1)}, f32[8,256]{1,0:T(8,128)S(1)}) custom-call(f32[3]{0:T(128)S(1)} %pad_maximum_fusion.scalars_ref.refs_0_, bf16[256,1920]{1,0:T(8,128)(2,1)S(1)} %shard_map.78.refs_1_, bf16[256,1920]{1,0:T(8,128)(2,1)S(1)} %collective-permute-done.1.refs_2_, ...), custom_call_target="tpu_custom_call" | custom-call | tf_op jit(solution)/shard_map/pallas_call | solution.py:67
  54.4 4.2 %collective-permute-done.8.refs_1_ = bf16[256,1920]{1,0:T(8,128)(2,1)S(1)} collective-permute-done((bf16[256,1920]{1,0:T(8,128)(2,1)S(1)}, bf16[256,1920]{1,0:T(8,128)(2,1)S(1)}, u32[]{:S(2)}, u32[]{:S(2)}) %collective-permute-start.8) | collective-permute-done | bytes 983072 | tf_op jit(solution)/shard_map/ppermute | solution.py:323
  58.6 0.1 collective-permute-done.9.in_ref
  58.8 0.3 collective-permute-start.10
  59.0 3.5 %shard_map.82 = (bf16[256,1920]{1,0:T(8,128)(2,1)S(1)}, bf16[1536,256]{1,0:T(8,128)(2,1)S(1)}, f32[8,256]{1,0:T(8,128)S(1)}) custom-call(f32[3]{0:T(128)S(1)} %pad_maximum_fusion.scalars_ref.refs_0_, bf16[256,1920]{1,0:T(8,128)(2,1)S(1)} %collective-permute-done.8.refs_1_, bf16[1536,1920]{1,0:T(8,128)(2,1)S(1)} %get-tuple-element.37.refs_2_), custom_call_target="tpu_custom_call" | custom-call | tf_op jit(solution)/shard_map/pallas_call | solution.py:67
  62.5 4.5 %shard_map.84 = (bf16[512,1920]{1,0:T(8,128)(2,1)S(1)}, bf16[512,1024]{1,0:T(8,128)(2,1)S(1)}, f32[8,256]{1,0:T(8,128)S(1)}) custom-call(f32[3]{0:T(128)S(1)} %pad_maximum_fusion.scalars_ref.refs_0_, bf16[256,1920]{1,0:T(8,128)(2,1)S(1)} %shard_map.83.refs_1_, bf16[256,1920]{1,0:T(8,128)(2,1)S(1)} %collective-permute-done.10.refs_2_, ...), custom_call_target="tpu_custom_call" | custom-call | tf_op jit(solution)/shard_map/pallas_call | solution.py:67
  67.1 2.1 %shard_map.85 = (bf16[272,1792]{1,0:T(8,128)(2,1)S(1)}, bf16[256,1792]{1,0:T(8,128)(2,1)S(1)}) custom-call(s32[1]{0:T(128)} %bitcast.1.core_ref.core, bf16[512,1024]{1,0:T(8,128)(2,1)S(1)} %get-tuple-element.43.refs_0_.refs_1_, bf16[512,1024]{1,0:T(8,128)(2,1)S(1)} %get-tuple-element.43.refs_0_.refs_1_, ...), custom_call_target="tpu_custom_call" | custom-call | tf_op jit(solution)/shard_map/pallas_call | solution.py:67
  69.2 0.6 collective-permute-start.11
  69.8 2.1 %shard_map.86.refs_3_ = bf16[256,1792]{1,0:T(8,128)(2,1)S(1)} custom-call(s32[1]{0:T(128)} %bitcast.1.core_ref.core, bf16[1536,256]{1,0:T(8,128)(2,1)S(1)} %get-tuple-element.38.refs_0_.refs_1_, bf16[512,1024]{1,0:T(8,128)(2,1)S(1)} %get-tuple-element.43.refs_0_.refs_1_, bf16[1536,1920]{1,0:T(8,128)(2,1)S(1)} %get-tuple-element.37.refs_2_, ...), custom_call_target="tpu_custom_call" | custom-call | tf_op jit(solution)/shard_map/pallas_call | solution.py:67
  72.0 0.5 shard_map.87
  72.5 2.1 %shard_map.88 = (bf16[256,1792]{1,0:T(8,128)(2,1)S(1)}, bf16[256,1792]{1,0:T(8,128)(2,1)S(1)}) custom-call(s32[1]{0:T(128)} %bitcast.1.core_ref.core, bf16[1536,768]{1,0:T(8,128)(2,1)S(1)} %get-tuple-element.35.refs_0_, bf16[1536,256]{1,0:T(8,128)(2,1)S(1)} %get-tuple-element.38.refs_0_.refs_1_, bf16[768,1920]{1,0:T(8,128)(2,1)S(1)} %get-tuple-element.39.refs_3_.refs_2_, ...), custom_call_target="tpu_custom_call" | custom-call | tf_op jit(solution)/shard_map/pallas_call | solution.py:67
  74.6 0.5 collective-permute-start.12
  75.0 0.3 collective-permute-start.17
  75.4 2.1 %shard_map.89.refs_2_ = bf16[256,1792]{1,0:T(8,128)(2,1)S(1)} custom-call(s32[1]{0:T(128)} %bitcast.1.core_ref.core, bf16[1536,768]{1,0:T(8,128)(2,1)S(1)} %get-tuple-element.35.refs_0_, bf16[512,1024]{1,0:T(8,128)(2,1)S(1)} %get-tuple-element.43.refs_0_.refs_1_, bf16[1536,1920]{1,0:T(8,128)(2,1)S(1)} %get-tuple-element.37.refs_2_, ...), custom_call_target="tpu_custom_call" | custom-call | tf_op jit(solution)/shard_map/pallas_call | solution.py:67
  77.5 3.0 %collective-permute-start.18 = (bf16[256,1792]{1,0:T(8,128)(2,1)S(1)}, bf16[256,1792]{1,0:T(8,128)(2,1)S(1)}, u32[]{:S(2)}, u32[]{:S(2)}) collective-permute-start(bf16[256,1792]{1,0:T(8,128)(2,1)S(1)} %shard_map.89.refs_2_), channel_id=1, source_target_pairs={{0,12},{2,6},{4,0},{6,10},{8,4},{10,14},{12,8},{14,2},{1,13},{3,7}... | collective-permute-start | bytes 2752520 | tf_op jit(solution)/shard_map/ppermute | solution.py:323
  80.5 0.2 shard_map.90.refs_4_
  80.7 3.3 %collective-permute-start.14 = (bf16[256,1792]{1,0:T(8,128)(2,1)S(1)}, bf16[256,1792]{1,0:T(8,128)(2,1)S(1)}, u32[]{:S(2)}, u32[]{:S(2)}) collective-permute-start(bf16[256,1792]{1,0:T(8,128)(2,1)S(1)} %shard_map.90.refs_4_), channel_id=1, source_target_pairs={{0,96},{2,34},{32,0},{34,66},{64,32},{66,98},{96,64},{98,2},{1,97}... | collective-permute-start | bytes 2752520 | tf_op jit(solution)/shard_map/ppermute | solution.py:323
  84.0 2.1 %shard_map.91 = (bf16[256,1792]{1,0:T(8,128)(2,1)S(1)}, bf16[256,1792]{1,0:T(8,128)(2,1)S(1)}) custom-call(s32[1]{0:T(128)} %bitcast.1.core_ref.core, bf16[1536,768]{1,0:T(8,128)(2,1)S(1)} %get-tuple-element.35.refs_0_, bf16[1536,256]{1,0:T(8,128)(2,1)S(1)} %get-tuple-element.38.refs_0_.refs_1_, bf16[768,1920]{1,0:T(8,128)(2,1)S(1)} %get-tuple-element.39.refs_3_.refs_2_, ...), custom_call_target="tpu_custom_call" | custom-call | tf_op jit(solution)/shard_map/pallas_call | solution.py:67
  86.1 2.1 %shard_map.92.refs_4_.refs_0_ = bf16[256,1792]{1,0:T(8,128)(2,1)S(1)} custom-call(s32[1]{0:T(128)} %bitcast.1.core_ref.core, bf16[1536,768]{1,0:T(8,128)(2,1)S(1)} %get-tuple-element.35.refs_0_, bf16[512,1024]{1,0:T(8,128)(2,1)S(1)} %get-tuple-element.43.refs_0_.refs_1_, bf16[1536,1920]{1,0:T(8,128)(2,1)S(1)} %get-tuple-element.37.refs_2_, ...), custom_call_target="tpu_custom_call" | custom-call | tf_op jit(solution)/shard_map/pallas_call | solution.py:67
  88.3 2.1 %shard_map.93 = (bf16[256,1792]{1,0:T(8,128)(2,1)S(1)}, bf16[256,1792]{1,0:T(8,128)(2,1)S(1)}) custom-call(s32[1]{0:T(128)} %bitcast.1.core_ref.core, bf16[1536,768]{1,0:T(8,128)(2,1)S(1)} %get-tuple-element.35.refs_0_, bf16[1536,256]{1,0:T(8,128)(2,1)S(1)} %get-tuple-element.38.refs_0_.refs_1_, bf16[768,1920]{1,0:T(8,128)(2,1)S(1)} %get-tuple-element.39.refs_3_.refs_2_, ...), custom_call_target="tpu_custom_call" | custom-call | tf_op jit(solution)/shard_map/pallas_call | solution.py:67
  90.4 0.1 collective-permute-start.13
  90.5 3.2 %collective-permute-done.17.refs_3_.refs_1_ = bf16[256,1792]{1,0:T(8,128)(2,1)S(1)} collective-permute-done((bf16[256,1792]{1,0:T(8,128)(2,1)S(1)}, bf16[256,1792]{1,0:T(8,128)(2,1)S(1)}, u32[]{:S(2)}, u32[]{:S(2)}) %collective-permute-start.17) | collective-permute-done | bytes 917536 | tf_op jit(solution)/shard_map/ppermute | solution.py:323
  93.7 1.3 collective-permute-start.15
  95.0 2.1 %shard_map.94.refs_6_.refs_5_.refs_0_ = bf16[256,1792]{1,0:T(8,128)(2,1)S(1)} custom-call(s32[1]{0:T(128)} %bitcast.1.core_ref.core, bf16[1536,768]{1,0:T(8,128)(2,1)S(1)} %get-tuple-element.35.refs_0_, bf16[512,1024]{1,0:T(8,128)(2,1)S(1)} %get-tuple-element.43.refs_0_.refs_1_, bf16[1536,1920]{1,0:T(8,128)(2,1)S(1)} %get-tuple-element.37.refs_2_, ...), custom_call_target="tpu_custom_call" | custom-call | tf_op jit(solution)/shard_map/pallas_call | solution.py:67
  97.2 0.9 collective-permute-done.18.refs_5_.refs_4_.refs_1_
  98.1 2.2 %collective-permute-done.14.refs_4_.refs_3_.refs_2_ = bf16[256,1792]{1,0:T(8,128)(2,1)S(1)} collective-permute-done((bf16[256,1792]{1,0:T(8,128)(2,1)S(1)}, bf16[256,1792]{1,0:T(8,128)(2,1)S(1)}, u32[]{:S(2)}, u32[]{:S(2)}) %collective-permute-start.14) | collective-permute-done | bytes 917536 | tf_op jit(solution)/shard_map/ppermute | solution.py:323
  100.3 0.2 shard_map.96.refs_1_
  100.6 0.3 shard_map.95.refs_0_
  101.1 3.0 %collective-permute-start.23 = (f32[8,128]{1,0:T(8,128)S(1)}, f32[8,128]{1,0:T(8,128)S(1)}, u32[]{:S(2)}, u32[]{:S(2)}) collective-permute-start(f32[8,128]{1,0:T(8,128)S(1)} %shard_map.97.refs_0_), channel_id=1, source_target_pairs={{0,17},{1,16},{16,1},{17,0},{2,19},{3,18},{18,3},{19,2},{4,21},{5,... | collective-permute-start | bytes 12296 | tf_op jit(solution)/shard_map/ppermute | solution.py:393
  104.1 1.7 %collective-permute-start.21 = (f32[8,128]{1,0:T(8,128)S(1)}, f32[8,128]{1,0:T(8,128)S(1)}, u32[]{:S(2)}, u32[]{:S(2)}) collective-permute-start(f32[8,128]{1,0:T(8,128)S(1)} %shard_map.97.refs_0_), channel_id=1, source_target_pairs={{0,1},{1,0},{16,17},{17,16},{2,3},{3,2},{18,19},{19,18},{4,5},{5,4... | collective-permute-start | bytes 12296 | tf_op jit(solution)/shard_map/ppermute | solution.py:393
  105.8 0.1 collective-permute-done.23.refs_3_
  106.0 1.7 %collective-permute-done.22.refs_2_ = f32[8,128]{1,0:T(8,128)S(1)} collective-permute-done((f32[8,128]{1,0:T(8,128)S(1)}, f32[8,128]{1,0:T(8,128)S(1)}, u32[]{:S(2)}, u32[]{:S(2)}) %collective-permute-start.22) | collective-permute-done | bytes 4128 | tf_op jit(solution)/shard_map/ppermute | solution.py:393
  107.7 1.5 %collective-permute-done.21.refs_1_ = f32[8,128]{1,0:T(8,128)S(1)} collective-permute-done((f32[8,128]{1,0:T(8,128)S(1)}, f32[8,128]{1,0:T(8,128)S(1)}, u32[]{:S(2)}, u32[]{:S(2)}) %collective-permute-start.21) | collective-permute-done | bytes 4128 | tf_op jit(solution)/shard_map/ppermute | solution.py:393
  109.2 6.0 %collective-permute-done.20.refs_2_ = bf16[256,1792]{1,0:T(8,128)(2,1)S(1)} collective-permute-done((bf16[256,1792]{1,0:T(8,128)(2,1)S(1)}, bf16[256,1792]{1,0:T(8,128)(2,1)S(1)}, u32[]{:S(2)}, u32[]{:S(2)}) %collective-permute-start.20) | collective-permute-done | bytes 917536 | tf_op jit(solution)/shard_map/ppermute | solution.py:323
  115.2 0.3 shard_map.99
  115.5 0.9 collective-permute-start.25
  116.5 0.4 shard_map.100
  116.9 3.9 %collective-permute-start.24 = (bf16[128,1792]{1,0:T(8,128)(2,1)S(1)}, bf16[128,1792]{1,0:T(8,128)(2,1)S(1)}, u32[]{:S(2)}, u32[]{:S(2)}) collective-permute-start(bf16[128,1792]{1,0:T(8,128)(2,1)S(1)} %get-tuple-element.59.refs_0_), channel_id=1, source_target_pairs={{0,1},{1,0},{2,3},{3,2},{4,5},{5,4},{6,7},{7,6},{8,9},{9,8},{10,11... | collective-permute-start | bytes 1376264 | tf_op jit(solution)/shard_map/ppermute | solution.py:328
  120.8 0.5 collective-permute-start.28
  121.3 1.0 collective-permute-start.27
  122.3 1.1 collective-permute-start.26
  123.3 2.6 %collective-permute-done.28.refs_3_ = f32[8,128]{1,0:T(8,128)S(1)} collective-permute-done((f32[8,128]{1,0:T(8,128)S(1)}, f32[8,128]{1,0:T(8,128)S(1)}, u32[]{:S(2)}, u32[]{:S(2)}) %collective-permute-start.28) | collective-permute-done | bytes 4128 | tf_op jit(solution)/shard_map/ppermute | solution.py:405
  125.9 1.2 collective-permute-done.26.refs_1_
  127.1 1.5 %collective-permute-start.31 = (f32[8,128]{1,0:T(8,128)S(1)}, f32[8,128]{1,0:T(8,128)S(1)}, u32[]{:S(2)}, u32[]{:S(2)}) collective-permute-start(f32[8,128]{1,0:T(8,128)S(1)} %shard_map.103.refs_0_), channel_id=1, source_target_pairs={{0,64},{32,96},{64,0},{96,32},{1,65},{33,97},{65,1},{97,33},{2,66}... | collective-permute-start | bytes 12296 | tf_op jit(solution)/shard_map/ppermute | solution.py:405
  128.6 1.6 %collective-permute-start.30 = (f32[8,128]{1,0:T(8,128)S(1)}, f32[8,128]{1,0:T(8,128)S(1)}, u32[]{:S(2)}, u32[]{:S(2)}) collective-permute-start(f32[8,128]{1,0:T(8,128)S(1)} %shard_map.103.refs_0_), channel_id=1, source_target_pairs={{0,96},{32,0},{64,32},{96,64},{1,97},{33,1},{65,33},{97,65},{2,98}... | collective-permute-start | bytes 12296 | tf_op jit(solution)/shard_map/ppermute | solution.py:405
  130.1 0.8 collective-permute-start.29
  130.9 1.3 collective-permute-done.31.refs_3_
  132.2 0.3 collective-permute-done.30.refs_2_
  132.5 2.4 %collective-permute-done.29.refs_1_ = f32[8,128]{1,0:T(8,128)S(1)} collective-permute-done((f32[8,128]{1,0:T(8,128)S(1)}, f32[8,128]{1,0:T(8,128)S(1)}, u32[]{:S(2)}, u32[]{:S(2)}) %collective-permute-start.29) | collective-permute-done | bytes 4128 | tf_op jit(solution)/shard_map/ppermute | solution.py:405
  135.0 0.5 slice.3
  136.2 1.6 %shard_map.101 = (bf16[128,1792]{1,0:T(8,128)(2,1)}, bf16[128,1792]{1,0:T(8,128)(2,1)}) custom-call(s32[1]{0:T(128)} %bitcast.pos_ref.half, bf16[256,1792]{1,0:T(8,128)(2,1)S(1)} %copy-done.1, bf16[256,1792]{1,0:T(8,128)(2,1)S(1)} %copy-done.3, f32[128,1792]{1,0:T(8,128)S(1)} %get-tuple-element.58.i_ref, ...), custom_call_target="tpu_custom_call" | custom-call | tf_op jit(solution)/shard_map/pallas_call | solution.py:67
  (41 shorter events, 0.7 us)
Async XLA Ops:
  0.6 1.2 copy-start.2
  1.8 0.7 copy-start.4
  2.7 8.9 %collective-permute-start = (bf16[128,1920]{1,0:T(8,128)(2,1)S(1)}, bf16[128,1920]{1,0:T(8,128)(2,1)S(1)}, u32[]{:S(2)}, u32[]{:S(2)}) collective-permute-start(bf16[128,1920]{1,0:T(8,128)(2,1)S(1)} %get-tuple-element.34.a_ref), channel_id=1, source_target_pairs={{0,16},{1,17},{2,19},{3,18},{16,0},{17,1},{18,3},{19,2},{4,20},{5,... | collective-permute-start | bytes 1474568 | tf_op jit(solution)/shard_map/ppermute | solution.py:337
  5.9 1.2 copy-start
  11.7 25.3 %collective-permute-start.4 = (bf16[256,1920]{1,0:T(8,128)(2,1)S(1)}, bf16[256,1920]{1,0:T(8,128)(2,1)S(1)}, u32[]{:S(2)}, u32[]{:S(2)}) collective-permute-start(bf16[256,1920]{1,0:T(8,128)(2,1)S(1)} %shard_map.78.refs_1_), channel_id=1, source_target_pairs={{0,96},{32,0},{64,32},{96,64},{1,97},{33,1},{65,33},{97,65},{2,98}... | collective-permute-start | bytes 2949128 | tf_op jit(solution)/shard_map/ppermute | solution.py:317
  15.9 24.6 %collective-permute-start.2 = (bf16[256,1920]{1,0:T(8,128)(2,1)S(1)}, bf16[256,1920]{1,0:T(8,128)(2,1)S(1)}, u32[]{:S(2)}, u32[]{:S(2)}) collective-permute-start(bf16[256,1920]{1,0:T(8,128)(2,1)S(1)} %shard_map.78.refs_1_), channel_id=1, source_target_pairs={{0,32},{32,64},{64,96},{96,0},{1,33},{33,65},{65,97},{97,1},{2,34}... | collective-permute-start | bytes 2949128 | tf_op jit(solution)/shard_map/ppermute | solution.py:317
  16.0 24.5 %collective-permute-start.7 = (bf16[256,1920]{1,0:T(8,128)(2,1)S(1)}, bf16[256,1920]{1,0:T(8,128)(2,1)S(1)}, u32[]{:S(2)}, u32[]{:S(2)}) collective-permute-start(bf16[256,1920]{1,0:T(8,128)(2,1)S(1)} %shard_map.79.refs_7_), channel_id=1, source_target_pairs={{0,12},{4,0},{8,4},{12,8},{1,13},{5,1},{9,5},{13,9},{2,14},{6,2},{... | collective-permute-start | bytes 2949128 | tf_op jit(solution)/shard_map/ppermute | solution.py:317
  18.8 24.3 %collective-permute-start.6 = (bf16[256,1920]{1,0:T(8,128)(2,1)S(1)}, bf16[256,1920]{1,0:T(8,128)(2,1)S(1)}, u32[]{:S(2)}, u32[]{:S(2)}) collective-permute-start(bf16[256,1920]{1,0:T(8,128)(2,1)S(1)} %shard_map.79.refs_7_), channel_id=1, source_target_pairs={{0,4},{4,8},{8,12},{12,0},{1,5},{5,9},{9,13},{13,1},{2,6},{6,10},{... | collective-permute-start | bytes 2949128 | tf_op jit(solution)/shard_map/ppermute | solution.py:317
  18.8 24.6 %collective-permute-start.1 = (bf16[256,1920]{1,0:T(8,128)(2,1)S(1)}, bf16[256,1920]{1,0:T(8,128)(2,1)S(1)}, u32[]{:S(2)}, u32[]{:S(2)}) collective-permute-start(bf16[256,1920]{1,0:T(8,128)(2,1)S(1)} %shard_map.78.refs_1_), channel_id=1, source_target_pairs={{0,2},{2,0},{1,3},{3,1},{4,6},{6,4},{5,7},{7,5},{8,10},{10,8},{9,1... | collective-permute-start | bytes 2949128 | tf_op jit(solution)/shard_map/ppermute | solution.py:328
  37.0 6.4 %collective-permute-start.5 = (bf16[256,1920]{1,0:T(8,128)(2,1)S(1)}, bf16[256,1920]{1,0:T(8,128)(2,1)S(1)}, u32[]{:S(2)}, u32[]{:S(2)}) collective-permute-start(bf16[256,1920]{1,0:T(8,128)(2,1)S(1)} %collective-permute-done.4.refs_5_.i_high), channel_id=1, source_target_pairs={{0,2},{2,0},{1,3},{3,1},{4,6},{6,4},{5,7},{7,5},{8,10},{10,8},{9,1... | collective-permute-start | bytes 2949128 | tf_op jit(solution)/shard_map/ppermute | solution.py:328
  40.5 3.0 %collective-permute-start.3 = (bf16[256,1920]{1,0:T(8,128)(2,1)S(1)}, bf16[256,1920]{1,0:T(8,128)(2,1)S(1)}, u32[]{:S(2)}, u32[]{:S(2)}) collective-permute-start(bf16[256,1920]{1,0:T(8,128)(2,1)S(1)} %collective-permute-done.2.refs_3_.i_low), channel_id=1, source_target_pairs={{0,2},{2,0},{1,3},{3,1},{4,6},{6,4},{5,7},{7,5},{8,10},{10,8},{9,1... | collective-permute-start | bytes 2949128 | tf_op jit(solution)/shard_map/ppermute | solution.py:328
  43.2 15.4 %collective-permute-start.8 = (bf16[256,1920]{1,0:T(8,128)(2,1)S(1)}, bf16[256,1920]{1,0:T(8,128)(2,1)S(1)}, u32[]{:S(2)}, u32[]{:S(2)}) collective-permute-start(bf16[256,1920]{1,0:T(8,128)(2,1)S(1)} %get-tuple-element.36), channel_id=1, source_target_pairs={{0,4},{2,14},{4,8},{6,2},{8,12},{10,6},{12,0},{14,10},{1,5},{3,15}... | collective-permute-start | bytes 2949128 | tf_op jit(solution)/shard_map/ppermute | solution.py:323
  43.3 15.4 %collective-permute-start.9 = (bf16[256,1920]{1,0:T(8,128)(2,1)S(1)}, bf16[256,1920]{1,0:T(8,128)(2,1)S(1)}, u32[]{:S(2)}, u32[]{:S(2)}) collective-permute-start(bf16[256,1920]{1,0:T(8,128)(2,1)S(1)} %get-tuple-element.41), channel_id=1, source_target_pairs={{0,32},{2,98},{32,64},{34,2},{64,96},{66,34},{96,0},{98,66},{1,33}... | collective-permute-start | bytes 2949128 | tf_op jit(solution)/shard_map/ppermute | solution.py:323
  58.8 3.8 %collective-permute-start.10 = (bf16[256,1920]{1,0:T(8,128)(2,1)S(1)}, bf16[256,1920]{1,0:T(8,128)(2,1)S(1)}, u32[]{:S(2)}, u32[]{:S(2)}) collective-permute-start(bf16[256,1920]{1,0:T(8,128)(2,1)S(1)} %shard_map.83.refs_1_), channel_id=1, source_target_pairs={{0,2},{2,0},{1,3},{3,1},{4,6},{6,4},{5,7},{7,5},{8,10},{10,8},{9,1... | collective-permute-start | bytes 2949128 | tf_op jit(solution)/shard_map/ppermute | solution.py:328
  69.2 2.8 %collective-permute-start.11 = (bf16[272,1792]{1,0:T(8,128)(2,1)S(1)}, bf16[272,1792]{1,0:T(8,128)(2,1)S(1)}, u32[]{:S(2)}, u32[]{:S(2)}) collective-permute-start(bf16[272,1792]{1,0:T(8,128)(2,1)S(1)} %get-tuple-element.48), channel_id=1, source_target_pairs={{0,2},{2,0},{1,3},{3,1},{4,6},{6,4},{5,7},{7,5},{8,10},{10,8},{9,1... | collective-permute-start | bytes 2924552 | tf_op jit(solution)/shard_map/ppermute | solution.py:328
  74.6 5.9 %collective-permute-start.12 = (bf16[256,1792]{1,0:T(8,128)(2,1)S(1)}, bf16[256,1792]{1,0:T(8,128)(2,1)S(1)}, u32[]{:S(2)}, u32[]{:S(2)}) collective-permute-start(bf16[256,1792]{1,0:T(8,128)(2,1)S(1)} %get-tuple-element.51), channel_id=1, source_target_pairs={{0,2},{2,0},{1,3},{3,1},{4,6},{6,4},{5,7},{7,5},{8,10},{10,8},{9,1... | collective-permute-start | bytes 2752520 | tf_op jit(solution)/shard_map/ppermute | solution.py:328
  75.0 18.6 %collective-permute-start.17 = (bf16[256,1792]{1,0:T(8,128)(2,1)S(1)}, bf16[256,1792]{1,0:T(8,128)(2,1)S(1)}, u32[]{:S(2)}, u32[]{:S(2)}) collective-permute-start(bf16[256,1792]{1,0:T(8,128)(2,1)S(1)} %shard_map.86.refs_3_), channel_id=1, source_target_pairs={{0,4},{2,14},{4,8},{6,2},{8,12},{10,6},{12,0},{14,10},{1,5},{3,15}... | collective-permute-start | bytes 2752520 | tf_op jit(solution)/shard_map/ppermute | solution.py:323
  75.4 21.8 %collective-permute-start.16 = (bf16[256,1792]{1,0:T(8,128)(2,1)S(1)}, bf16[256,1792]{1,0:T(8,128)(2,1)S(1)}, u32[]{:S(2)}, u32[]{:S(2)}) collective-permute-start(bf16[256,1792]{1,0:T(8,128)(2,1)S(1)} %get-tuple-element.49.refs_4_), channel_id=1, source_target_pairs={{0,32},{2,98},{32,64},{34,2},{64,96},{66,34},{96,0},{98,66},{1,33}... | collective-permute-start | bytes 2752520 | tf_op jit(solution)/shard_map/ppermute | solution.py:323
  77.5 20.6 %collective-permute-start.18 = (bf16[256,1792]{1,0:T(8,128)(2,1)S(1)}, bf16[256,1792]{1,0:T(8,128)(2,1)S(1)}, u32[]{:S(2)}, u32[]{:S(2)}) collective-permute-start(bf16[256,1792]{1,0:T(8,128)(2,1)S(1)} %shard_map.89.refs_2_), channel_id=1, source_target_pairs={{0,12},{2,6},{4,0},{6,10},{8,4},{10,14},{12,8},{14,2},{1,13},{3,7}... | collective-permute-start | bytes 2752520 | tf_op jit(solution)/shard_map/ppermute | solution.py:323
  80.7 19.6 %collective-permute-start.14 = (bf16[256,1792]{1,0:T(8,128)(2,1)S(1)}, bf16[256,1792]{1,0:T(8,128)(2,1)S(1)}, u32[]{:S(2)}, u32[]{:S(2)}) collective-permute-start(bf16[256,1792]{1,0:T(8,128)(2,1)S(1)} %shard_map.90.refs_4_), channel_id=1, source_target_pairs={{0,96},{2,34},{32,0},{34,66},{64,32},{66,98},{96,64},{98,2},{1,97}... | collective-permute-start | bytes 2752520 | tf_op jit(solution)/shard_map/ppermute | solution.py:323
  90.4 10.2 %collective-permute-start.13 = (bf16[256,1792]{1,0:T(8,128)(2,1)S(1)}, bf16[256,1792]{1,0:T(8,128)(2,1)S(1)}, u32[]{:S(2)}, u32[]{:S(2)}) collective-permute-start(bf16[256,1792]{1,0:T(8,128)(2,1)S(1)} %get-tuple-element.54), channel_id=1, source_target_pairs={{0,2},{2,0},{1,3},{3,1},{4,6},{6,4},{5,7},{7,5},{8,10},{10,8},{9,1... | collective-permute-start | bytes 2752520 | tf_op jit(solution)/shard_map/ppermute | solution.py:328
  93.7 6.9 %collective-permute-start.15 = (bf16[256,1792]{1,0:T(8,128)(2,1)S(1)}, bf16[256,1792]{1,0:T(8,128)(2,1)S(1)}, u32[]{:S(2)}, u32[]{:S(2)}) collective-permute-start(bf16[256,1792]{1,0:T(8,128)(2,1)S(1)} %get-tuple-element.55), channel_id=1, source_target_pairs={{0,2},{2,0},{1,3},{3,1},{4,6},{6,4},{5,7},{7,5},{8,10},{10,8},{9,1... | collective-permute-start | bytes 2752520 | tf_op jit(solution)/shard_map/ppermute | solution.py:328
  100.5 14.7 %collective-permute-start.20 = (bf16[256,1792]{1,0:T(8,128)(2,1)S(1)}, bf16[256,1792]{1,0:T(8,128)(2,1)S(1)}, u32[]{:S(2)}, u32[]{:S(2)}) collective-permute-start(bf16[256,1792]{1,0:T(8,128)(2,1)S(1)} %shard_map.96.refs_1_), channel_id=1, source_target_pairs={{0,4},{2,14},{4,8},{6,2},{8,12},{10,6},{12,0},{14,10},{1,5},{3,15}... | collective-permute-start | bytes 2752520 | tf_op jit(solution)/shard_map/ppermute | solution.py:323
  101.0 15.5 %collective-permute-start.19 = (bf16[256,1792]{1,0:T(8,128)(2,1)S(1)}, bf16[256,1792]{1,0:T(8,128)(2,1)S(1)}, u32[]{:S(2)}, u32[]{:S(2)}) collective-permute-start(bf16[256,1792]{1,0:T(8,128)(2,1)S(1)} %shard_map.95.refs_0_), channel_id=1, source_target_pairs={{0,32},{2,98},{32,64},{34,2},{64,96},{66,34},{96,0},{98,66},{1,33}... | collective-permute-start | bytes 2752520 | tf_op jit(solution)/shard_map/ppermute | solution.py:323
  101.1 4.9 %collective-permute-start.23 = (f32[8,128]{1,0:T(8,128)S(1)}, f32[8,128]{1,0:T(8,128)S(1)}, u32[]{:S(2)}, u32[]{:S(2)}) collective-permute-start(f32[8,128]{1,0:T(8,128)S(1)} %shard_map.97.refs_0_), channel_id=1, source_target_pairs={{0,17},{1,16},{16,1},{17,0},{2,19},{3,18},{18,3},{19,2},{4,21},{5,... | collective-permute-start | bytes 12296 | tf_op jit(solution)/shard_map/ppermute | solution.py:393
  104.1 3.6 %collective-permute-start.22 = (f32[8,128]{1,0:T(8,128)S(1)}, f32[8,128]{1,0:T(8,128)S(1)}, u32[]{:S(2)}, u32[]{:S(2)}) collective-permute-start(f32[8,128]{1,0:T(8,128)S(1)} %shard_map.97.refs_0_), channel_id=1, source_target_pairs={{0,16},{1,17},{16,0},{17,1},{2,18},{3,19},{18,2},{19,3},{4,20},{5,... | collective-permute-start | bytes 12296 | tf_op jit(solution)/shard_map/ppermute | solution.py:393
  104.1 5.1 %collective-permute-start.21 = (f32[8,128]{1,0:T(8,128)S(1)}, f32[8,128]{1,0:T(8,128)S(1)}, u32[]{:S(2)}, u32[]{:S(2)}) collective-permute-start(f32[8,128]{1,0:T(8,128)S(1)} %shard_map.97.refs_0_), channel_id=1, source_target_pairs={{0,1},{1,0},{16,17},{17,16},{2,3},{3,2},{18,19},{19,18},{4,5},{5,4... | collective-permute-start | bytes 12296 | tf_op jit(solution)/shard_map/ppermute | solution.py:393
  115.5 20.6 %copy-start.1 = (bf16[256,1792]{1,0:T(8,128)(2,1)S(1)}, bf16[256,1792]{1,0:T(8,128)(2,1)}, u32[]{:S(2)}) copy-start(bf16[256,1792]{1,0:T(8,128)(2,1)} %img_ref.3) | copy-start | bytes 2752516
  115.5 20.6 %copy-start.3 = (bf16[256,1792]{1,0:T(8,128)(2,1)S(1)}, bf16[256,1792]{1,0:T(8,128)(2,1)}, u32[]{:S(2)}) copy-start(bf16[256,1792]{1,0:T(8,128)(2,1)} %txt_ref.3) | copy-start | bytes 2752516
  115.5 20.6 %collective-permute-start.25 = (bf16[128,1792]{1,0:T(8,128)(2,1)S(1)}, bf16[128,1792]{1,0:T(8,128)(2,1)S(1)}, u32[]{:S(2)}, u32[]{:S(2)}) collective-permute-start(bf16[128,1792]{1,0:T(8,128)(2,1)S(1)} %get-tuple-element.57.refs_4_), channel_id=1, source_target_pairs={{0,16},{1,17},{2,19},{3,18},{16,0},{17,1},{18,3},{19,2},{4,20},{5,... | collective-permute-start | bytes 1376264 | tf_op jit(solution)/shard_map/ppermute | solution.py:337
  116.9 19.2 %collective-permute-start.24 = (bf16[128,1792]{1,0:T(8,128)(2,1)S(1)}, bf16[128,1792]{1,0:T(8,128)(2,1)S(1)}, u32[]{:S(2)}, u32[]{:S(2)}) collective-permute-start(bf16[128,1792]{1,0:T(8,128)(2,1)S(1)} %get-tuple-element.59.refs_0_), channel_id=1, source_target_pairs={{0,1},{1,0},{2,3},{3,2},{4,5},{5,4},{6,7},{7,6},{8,9},{9,8},{10,11... | collective-permute-start | bytes 1376264 | tf_op jit(solution)/shard_map/ppermute | solution.py:328
  120.8 5.1 %collective-permute-start.28 = (f32[8,128]{1,0:T(8,128)S(1)}, f32[8,128]{1,0:T(8,128)S(1)}, u32[]{:S(2)}, u32[]{:S(2)}) collective-permute-start(f32[8,128]{1,0:T(8,128)S(1)} %shard_map.102.refs_0_), channel_id=1, source_target_pairs={{0,8},{4,12},{8,0},{12,4},{1,9},{5,13},{9,1},{13,5},{2,10},{6,14},... | collective-permute-start | bytes 12296 | tf_op jit(solution)/shard_map/ppermute | solution.py:405
  121.3 4.6 %collective-permute-start.27 = (f32[8,128]{1,0:T(8,128)S(1)}, f32[8,128]{1,0:T(8,128)S(1)}, u32[]{:S(2)}, u32[]{:S(2)}) collective-permute-start(f32[8,128]{1,0:T(8,128)S(1)} %shard_map.102.refs_0_), channel_id=1, source_target_pairs={{0,12},{4,0},{8,4},{12,8},{1,13},{5,1},{9,5},{13,9},{2,14},{6,2},{... | collective-permute-start | bytes 12296 | tf_op jit(solution)/shard_map/ppermute | solution.py:405
  122.3 4.8 %collective-permute-start.26 = (f32[8,128]{1,0:T(8,128)S(1)}, f32[8,128]{1,0:T(8,128)S(1)}, u32[]{:S(2)}, u32[]{:S(2)}) collective-permute-start(f32[8,128]{1,0:T(8,128)S(1)} %shard_map.102.refs_0_), channel_id=1, source_target_pairs={{0,4},{4,8},{8,12},{12,0},{1,5},{5,9},{9,13},{13,1},{2,6},{6,10},{... | collective-permute-start | bytes 12296 | tf_op jit(solution)/shard_map/ppermute | solution.py:405
  127.1 5.1 %collective-permute-start.31 = (f32[8,128]{1,0:T(8,128)S(1)}, f32[8,128]{1,0:T(8,128)S(1)}, u32[]{:S(2)}, u32[]{:S(2)}) collective-permute-start(f32[8,128]{1,0:T(8,128)S(1)} %shard_map.103.refs_0_), channel_id=1, source_target_pairs={{0,64},{32,96},{64,0},{96,32},{1,65},{33,97},{65,1},{97,33},{2,66}... | collective-permute-start | bytes 12296 | tf_op jit(solution)/shard_map/ppermute | solution.py:405
  128.6 4.0 %collective-permute-start.30 = (f32[8,128]{1,0:T(8,128)S(1)}, f32[8,128]{1,0:T(8,128)S(1)}, u32[]{:S(2)}, u32[]{:S(2)}) collective-permute-start(f32[8,128]{1,0:T(8,128)S(1)} %shard_map.103.refs_0_), channel_id=1, source_target_pairs={{0,96},{32,0},{64,32},{96,64},{1,97},{33,1},{65,33},{97,65},{2,98}... | collective-permute-start | bytes 12296 | tf_op jit(solution)/shard_map/ppermute | solution.py:405
  130.1 4.8 %collective-permute-start.29 = (f32[8,128]{1,0:T(8,128)S(1)}, f32[8,128]{1,0:T(8,128)S(1)}, u32[]{:S(2)}, u32[]{:S(2)}) collective-permute-start(f32[8,128]{1,0:T(8,128)S(1)} %shard_map.103.refs_0_), channel_id=1, source_target_pairs={{0,32},{32,64},{64,96},{96,0},{1,33},{33,65},{65,97},{97,1},{2,34}... | collective-permute-start | bytes 12296 | tf_op jit(solution)/shard_map/ppermute | solution.py:405
where the time goes:
time: 139 us
  waiting for transfers between devices  55.8 us (40%)
  Pallas kernels  41 us (29%)
  starting transfers between devices  34.3 us (25%)
  between operations  4.09 us (3%)
  local copies, waits for them, and re-layouts  3.56 us (3%)
    pallas_call x29, Pallas kernels, kernel_call(): pl.pallas_call(body, in_specs=specs, out_specs=[VM] * len(outs), out_shap...  41 us
    ppermute x2, waiting for transfers between devices, both_ways(): lax.ppermute(value, axis, ring(axis, -1))  18.2 us
    ppermute x8, waiting for transfers between devices, by_core(): return lax.ppermute(value, (axis, 'c'), perm)  16.6 us
    ppermute x6, waiting for transfers between devices, local(): lax.ppermute(loss, axis, ring(axis, by))  7.79 us
    ppermute x2, starting transfers between devices, both_ways(): lax.ppermute(value, axis, ring(axis, -1))  7.02 us
    ppermute x8, starting transfers between devices, by_core(): return lax.ppermute(value, (axis, 'c'), perm)  6.91 us
    ppermute x9, starting transfers between devices, swapped(): return lax.ppermute(value, axis, [(i, i ^ bit) for i in range(n)])  6.6 us
    ppermute x6, starting transfers between devices, local(): lax.ppermute(loss, axis, ring(axis, by))  6.34 us
  transfers between devices with their start and end apart: 32, of which 18 were waited for; matrix products, arithmetic and copies ran while one was open for 0% of the time, Pallas kernels for 21%

commit v1 on v0

--- a/solution.py
+++ b/solution.py
@@ -368,19 +368,19 @@
     i_far, p_rows, loss_c = logits(scalars, (i_far, i_far_s), (), (), (t_near, t_far))
     losses, texts, images = (loss_a, loss_b, loss_c), (t_near, t_far), (i_near, i_far)
     far_s, far = image_grads(core, (1, 0), (p_rows, p_rows), texts, losses)
-    (t_far,) = text_grads(core, ((0, 3),), (p_cols, p_rows), images, ties=(far,))
+    near_parts, near_texts = (p_near, p_cols), (p_near, p_rows)
+    two_s, one = image_grads(core, ((5, 3), (2, 4)), near_parts, texts, ties=(far,))
+    (t_far,) = text_grads(core, ((0, 3),), (p_cols, p_rows), images, ties=(one,))
     t_got = by_core(t_far, "x")
     z_far, loss = kernel_call(
         far_kernel, (far, swapped(far_s, "c"), *losses), [((ROWS, E), bf16), ((8, 128), f32)], ties=(t_far,)
     )
     z_got = by_core(z_far, "z")
-    near_parts, near_texts = (p_near, p_cols), (p_near, p_rows)
-    two_s, one = image_grads(core, ((5, 3), (2, 4)), near_parts, texts, ties=(z_far,))
-    (t_one,) = text_grads(core, (((1, 2), (1, 2)),), near_texts, images, ties=(one,))
+    z_one = near((one, swapped(two_s, "c")), ties=(z_far,))
+    z_from_one = by_core(z_one, "z", -1)
+    (t_one,) = text_grads(core, (((1, 2), (1, 2)),), near_texts, images, ties=(z_one,))
     t_from_one = by_core(t_one, "x", -1)
-    z_one = near((one, swapped(two_s, "c")), ties=(t_one,))
-    z_from_one = by_core(z_one, "z", -1)
-    one_s, two = image_grads(core, ((3, 5), (4, 2)), near_parts, texts, ties=(z_one,))
+    one_s, two = image_grads(core, ((3, 5), (4, 2)), near_parts, texts, ties=(t_one,))
     (t_two,) = text_grads(core, (((2, 1), (2, 1)),), near_texts, images, ties=(two,))
     own_s, own = image_grads(core, (1, 0), near_parts, texts, ties=(t_two,))
     (t_own,) = text_grads(core, ((0, 0),), near_texts, images, ties=(own,))

time: 139 us -> 140 us (level)
  waiting for transfers between devices: 55.8 us -> 58.1 us
  starting transfers between devices: 34.3 us -> 32.5 us
    ppermute x8, waiting for transfers between devices: 16.6 us -> 18.4 us  [by_core(): return lax.ppermute(value, (axis, 'c'), perm)]
    ppermute x9, starting transfers between devices: 6.6 us -> 4.91 us  [swapped(): return lax.ppermute(value, axis, [(i, i ^ bit) for i in range(n)])]
  transfers between devices with their start and end apart: 32 -> 32, of which waited for: 18 -> 19; matrix products, arithmetic and copies ran while one was open for 0% -> 0% of each run, Pallas kernels for 21% -> 23%
where the time goes in v1:
time: 140 us; the launch traced here: 139 us
  waiting for transfers between devices  58.1 us (42%)
  Pallas kernels  41 us (29%)
  starting transfers between devices  32.5 us (23%)
  between operations  4.11 us (3%)
  local copies, waits for them, and re-layouts  3.56 us (3%)
    pallas_call x29, Pallas kernels, kernel_call(): pl.pallas_call(body, in_specs=specs, out_specs=[VM] * len(outs), out_shap...  41 us
    ppermute x8, waiting for transfers between devices, by_core(): return lax.ppermute(value, (axis, 'c'), perm)  18.4 us
    ppermute x2, waiting for transfers between devices, both_ways(): lax.ppermute(value, axis, ring(axis, -1))  18.2 us
    ppermute x6, waiting for transfers between devices, local(): lax.ppermute(loss, axis, ring(axis, by))  8.37 us
    ppermute x8, starting transfers between devices, by_core(): return lax.ppermute(value, (axis, 'c'), perm)  7.18 us
    ppermute x2, starting transfers between devices, both_ways(): lax.ppermute(value, axis, ring(axis, -1))  7.02 us
    ppermute x2, waiting for transfers between devices, both_ways(): lax.ppermute(value, axis, ring(axis, 1))  6.03 us
    ppermute x6, starting transfers between devices, local(): lax.ppermute(loss, axis, ring(axis, by))  5.9 us
  transfers between devices with their start and end apart: 32, of which 19 were waited for; matrix products, arithmetic and copies ran while one was open for 0% of the time, Pallas kernels for 23%

profile of v1, /device:TPU:0, one launch (start us, length us, event | category | flops | bytes accessed | tf_op | source)
XLA Modules:
  0.0 139.3 jit_solution(13128986947959095768)
XLA Ops:
  0.6 1.2 copy-done.2
  1.8 0.7 copy-done.4
  2.5 0.2 shard_map.76
  2.7 1.7 %collective-permute-start = (bf16[128,1920]{1,0:T(8,128)(2,1)S(1)}, bf16[128,1920]{1,0:T(8,128)(2,1)S(1)}, u32[]{:S(2)}, u32[]{:S(2)}) collective-permute-start(bf16[128,1920]{1,0:T(8,128)(2,1)S(1)} %get-tuple-element.34.a_ref), channel_id=1, source_target_pairs={{0,16},{1,17},{2,19},{3,18},{16,0},{17,1},{18,3},{19,2},{4,20},{5,... | collective-permute-start | bytes 1474568 | tf_op jit(solution)/shard_map/ppermute | solution.py:337
  5.9 1.2 copy-done
  7.1 0.8 shard_map.77.in_ref
  7.9 3.7 %collective-permute-done.refs_0_.b_ref = bf16[128,1920]{1,0:T(8,128)(2,1)S(1)} collective-permute-done((bf16[128,1920]{1,0:T(8,128)(2,1)S(1)}, bf16[128,1920]{1,0:T(8,128)(2,1)S(1)}, u32[]{:S(2)}, u32[]{:S(2)}) %collective-permute-start) | collective-permute-done | bytes 491552 | tf_op jit(solution)/shard_map/ppermute | solution.py:337
  11.7 4.2 %collective-permute-start.4 = (bf16[256,1920]{1,0:T(8,128)(2,1)S(1)}, bf16[256,1920]{1,0:T(8,128)(2,1)S(1)}, u32[]{:S(2)}, u32[]{:S(2)}) collective-permute-start(bf16[256,1920]{1,0:T(8,128)(2,1)S(1)} %shard_map.78.refs_1_), channel_id=1, source_target_pairs={{0,96},{32,0},{64,32},{96,64},{1,97},{33,1},{65,33},{97,65},{2,98}... | collective-permute-start | bytes 2949128 | tf_op jit(solution)/shard_map/ppermute | solution.py:317
  16.0 2.8 %collective-permute-start.7 = (bf16[256,1920]{1,0:T(8,128)(2,1)S(1)}, bf16[256,1920]{1,0:T(8,128)(2,1)S(1)}, u32[]{:S(2)}, u32[]{:S(2)}) collective-permute-start(bf16[256,1920]{1,0:T(8,128)(2,1)S(1)} %shard_map.79.refs_7_), channel_id=1, source_target_pairs={{0,12},{4,0},{8,4},{12,8},{1,13},{5,1},{9,5},{13,9},{2,14},{6,2},{... | collective-permute-start | bytes 2949128 | tf_op jit(solution)/shard_map/ppermute | solution.py:317
  18.8 18.2 %collective-permute-done.4.refs_5_.i_high = bf16[256,1920]{1,0:T(8,128)(2,1)S(1)} collective-permute-done((bf16[256,1920]{1,0:T(8,128)(2,1)S(1)}, bf16[256,1920]{1,0:T(8,128)(2,1)S(1)}, u32[]{:S(2)}, u32[]{:S(2)}) %collective-permute-start.4) | collective-permute-done | bytes 983072 | tf_op jit(solution)/shard_map/ppermute | solution.py:317
  37.0 3.4 %collective-permute-done.2.refs_3_.i_low = bf16[256,1920]{1,0:T(8,128)(2,1)S(1)} collective-permute-done((bf16[256,1920]{1,0:T(8,128)(2,1)S(1)}, bf16[256,1920]{1,0:T(8,128)(2,1)S(1)}, u32[]{:S(2)}, u32[]{:S(2)}) %collective-permute-start.2) | collective-permute-done | bytes 983072 | tf_op jit(solution)/shard_map/ppermute | solution.py:317
  40.5 2.6 %collective-permute-done.6.refs_8_.t_low = bf16[256,1920]{1,0:T(8,128)(2,1)S(1)} collective-permute-done((bf16[256,1920]{1,0:T(8,128)(2,1)S(1)}, bf16[256,1920]{1,0:T(8,128)(2,1)S(1)}, u32[]{:S(2)}, u32[]{:S(2)}) %collective-permute-start.6) | collective-permute-done | bytes 983072 | tf_op jit(solution)/shard_map/ppermute | solution.py:317
  43.1 0.1 shard_map.81
  43.4 10.9 %shard_map.80 = (bf16[1536,1920]{1,0:T(8,128)(2,1)S(1)}, bf16[768,1920]{1,0:T(8,128)(2,1)S(1)}, bf16[1536,768]{1,0:T(8,128)(2,1)S(1)}, f32[8,256]{1,0:T(8,128)S(1)}) custom-call(f32[3]{0:T(128)S(1)} %pad_maximum_fusion.scalars_ref.refs_0_, bf16[256,1920]{1,0:T(8,128)(2,1)S(1)} %shard_map.78.refs_1_, bf16[256,1920]{1,0:T(8,128)(2,1)S(1)} %collective-permute-done.1.refs_2_, ...), custom_call_target="tpu_custom_call" | custom-call | tf_op jit(solution)/shard_map/pallas_call | solution.py:67
  54.4 4.2 %collective-permute-done.8.refs_1_ = bf16[256,1920]{1,0:T(8,128)(2,1)S(1)} collective-permute-done((bf16[256,1920]{1,0:T(8,128)(2,1)S(1)}, bf16[256,1920]{1,0:T(8,128)(2,1)S(1)}, u32[]{:S(2)}, u32[]{:S(2)}) %collective-permute-start.8) | collective-permute-done | bytes 983072 | tf_op jit(solution)/shard_map/ppermute | solution.py:323
  58.6 0.1 collective-permute-done.9.in_ref
  58.8 0.3 collective-permute-start.10
  59.0 3.5 %shard_map.82 = (bf16[256,1920]{1,0:T(8,128)(2,1)S(1)}, bf16[1536,256]{1,0:T(8,128)(2,1)S(1)}, f32[8,256]{1,0:T(8,128)S(1)}) custom-call(f32[3]{0:T(128)S(1)} %pad_maximum_fusion.scalars_ref.refs_0_, bf16[256,1920]{1,0:T(8,128)(2,1)S(1)} %collective-permute-done.8.refs_1_, bf16[1536,1920]{1,0:T(8,128)(2,1)S(1)} %get-tuple-element.37.refs_2_), custom_call_target="tpu_custom_call" | custom-call | tf_op jit(solution)/shard_map/pallas_call | solution.py:67
  62.5 4.5 %shard_map.84 = (bf16[512,1920]{1,0:T(8,128)(2,1)S(1)}, bf16[512,1024]{1,0:T(8,128)(2,1)S(1)}, f32[8,256]{1,0:T(8,128)S(1)}) custom-call(f32[3]{0:T(128)S(1)} %pad_maximum_fusion.scalars_ref.refs_0_, bf16[256,1920]{1,0:T(8,128)(2,1)S(1)} %shard_map.83.refs_1_, bf16[256,1920]{1,0:T(8,128)(2,1)S(1)} %collective-permute-done.10.refs_2_, ...), custom_call_target="tpu_custom_call" | custom-call | tf_op jit(solution)/shard_map/pallas_call | solution.py:67
  67.1 2.1 %shard_map.85 = (bf16[272,1792]{1,0:T(8,128)(2,1)S(1)}, bf16[256,1792]{1,0:T(8,128)(2,1)S(1)}) custom-call(s32[1]{0:T(128)} %bitcast.1.core_ref.core, bf16[512,1024]{1,0:T(8,128)(2,1)S(1)} %get-tuple-element.43.refs_0_.refs_1_, bf16[512,1024]{1,0:T(8,128)(2,1)S(1)} %get-tuple-element.43.refs_0_.refs_1_, ...), custom_call_target="tpu_custom_call" | custom-call | tf_op jit(solution)/shard_map/pallas_call | solution.py:67
  69.2 0.6 collective-permute-start.12
  69.8 2.1 %shard_map.86 = (bf16[256,1792]{1,0:T(8,128)(2,1)S(1)}, bf16[256,1792]{1,0:T(8,128)(2,1)S(1)}) custom-call(s32[1]{0:T(128)} %bitcast.1.core_ref.core, bf16[1536,768]{1,0:T(8,128)(2,1)S(1)} %get-tuple-element.35.refs_0_, bf16[1536,256]{1,0:T(8,128)(2,1)S(1)} %get-tuple-element.38.refs_1_.refs_0_, bf16[768,1920]{1,0:T(8,128)(2,1)S(1)} %get-tuple-element.39.refs_3_.refs_2_, ...), custom_call_target="tpu_custom_call" | custom-call | tf_op jit(solution)/shard_map/pallas_call | solution.py:67
  71.9 0.1 collective-permute-start.11
  72.0 2.1 %shard_map.87.refs_3_ = bf16[256,1792]{1,0:T(8,128)(2,1)S(1)} custom-call(s32[1]{0:T(128)} %bitcast.1.core_ref.core, bf16[1536,256]{1,0:T(8,128)(2,1)S(1)} %get-tuple-element.38.refs_1_.refs_0_, bf16[512,1024]{1,0:T(8,128)(2,1)S(1)} %get-tuple-element.43.refs_0_.refs_1_, bf16[1536,1920]{1,0:T(8,128)(2,1)S(1)} %get-tuple-element.37.refs_2_, ...), custom_call_target="tpu_custom_call" | custom-call | tf_op jit(solution)/shard_map/pallas_call | solution.py:67
  74.1 0.4 collective-permute-start.17
  74.5 0.5 shard_map.88
  75.0 0.3 collective-permute-start.16
  75.3 0.2 shard_map.89.refs_4_
  75.6 2.1 %shard_map.90.refs_4_ = bf16[256,1792]{1,0:T(8,128)(2,1)S(1)} custom-call(s32[1]{0:T(128)} %bitcast.1.core_ref.core, bf16[1536,768]{1,0:T(8,128)(2,1)S(1)} %get-tuple-element.35.refs_0_, bf16[512,1024]{1,0:T(8,128)(2,1)S(1)} %get-tuple-element.43.refs_0_.refs_1_, bf16[1536,1920]{1,0:T(8,128)(2,1)S(1)} %get-tuple-element.37.refs_2_, ...), custom_call_target="tpu_custom_call" | custom-call | tf_op jit(solution)/shard_map/pallas_call | solution.py:67
  77.7 3.3 %collective-permute-start.14 = (bf16[256,1792]{1,0:T(8,128)(2,1)S(1)}, bf16[256,1792]{1,0:T(8,128)(2,1)S(1)}, u32[]{:S(2)}, u32[]{:S(2)}) collective-permute-start(bf16[256,1792]{1,0:T(8,128)(2,1)S(1)} %shard_map.89.refs_4_), channel_id=1, source_target_pairs={{0,96},{2,34},{32,0},{34,66},{64,32},{66,98},{96,64},{98,2},{1,97}... | collective-permute-start | bytes 2752520 | tf_op jit(solution)/shard_map/ppermute | solution.py:323
  81.0 2.9 %collective-permute-start.18 = (bf16[256,1792]{1,0:T(8,128)(2,1)S(1)}, bf16[256,1792]{1,0:T(8,128)(2,1)S(1)}, u32[]{:S(2)}, u32[]{:S(2)}) collective-permute-start(bf16[256,1792]{1,0:T(8,128)(2,1)S(1)} %shard_map.90.refs_4_), channel_id=1, source_target_pairs={{0,12},{2,6},{4,0},{6,10},{8,4},{10,14},{12,8},{14,2},{1,13},{3,7}... | collective-permute-start | bytes 2752520 | tf_op jit(solution)/shard_map/ppermute | solution.py:323
  83.9 2.1 %shard_map.91 = (bf16[256,1792]{1,0:T(8,128)(2,1)S(1)}, bf16[256,1792]{1,0:T(8,128)(2,1)S(1)}) custom-call(s32[1]{0:T(128)} %bitcast.1.core_ref.core, bf16[1536,768]{1,0:T(8,128)(2,1)S(1)} %get-tuple-element.35.refs_0_, bf16[1536,256]{1,0:T(8,128)(2,1)S(1)} %get-tuple-element.38.refs_1_.refs_0_, bf16[768,1920]{1,0:T(8,128)(2,1)S(1)} %get-tuple-element.39.refs_3_.refs_2_, ...), custom_call_target="tpu_custom_call" | custom-call | tf_op jit(solution)/shard_map/pallas_call | solution.py:67
  86.0 2.1 %shard_map.92.refs_4_.refs_0_ = bf16[256,1792]{1,0:T(8,128)(2,1)S(1)} custom-call(s32[1]{0:T(128)} %bitcast.1.core_ref.core, bf16[1536,768]{1,0:T(8,128)(2,1)S(1)} %get-tuple-element.35.refs_0_, bf16[512,1024]{1,0:T(8,128)(2,1)S(1)} %get-tuple-element.43.refs_0_.refs_1_, bf16[1536,1920]{1,0:T(8,128)(2,1)S(1)} %get-tuple-element.37.refs_2_, ...), custom_call_target="tpu_custom_call" | custom-call | tf_op jit(solution)/shard_map/pallas_call | solution.py:67
  88.2 2.1 %shard_map.93 = (bf16[256,1792]{1,0:T(8,128)(2,1)S(1)}, bf16[256,1792]{1,0:T(8,128)(2,1)S(1)}) custom-call(s32[1]{0:T(128)} %bitcast.1.core_ref.core, bf16[1536,768]{1,0:T(8,128)(2,1)S(1)} %get-tuple-element.35.refs_0_, bf16[1536,256]{1,0:T(8,128)(2,1)S(1)} %get-tuple-element.38.refs_1_.refs_0_, bf16[768,1920]{1,0:T(8,128)(2,1)S(1)} %get-tuple-element.39.refs_3_.refs_2_, ...), custom_call_target="tpu_custom_call" | custom-call | tf_op jit(solution)/shard_map/pallas_call | solution.py:67
  90.3 0.1 collective-permute-start.13
  90.4 1.0 collective-permute-done.17.refs_3_.refs_1_
  91.4 2.1 %shard_map.94.refs_6_.refs_5_.refs_0_ = bf16[256,1792]{1,0:T(8,128)(2,1)S(1)} custom-call(s32[1]{0:T(128)} %bitcast.1.core_ref.core, bf16[1536,768]{1,0:T(8,128)(2,1)S(1)} %get-tuple-element.35.refs_0_, bf16[512,1024]{1,0:T(8,128)(2,1)S(1)} %get-tuple-element.43.refs_0_.refs_1_, bf16[1536,1920]{1,0:T(8,128)(2,1)S(1)} %get-tuple-element.37.refs_2_, ...), custom_call_target="tpu_custom_call" | custom-call | tf_op jit(solution)/shard_map/pallas_call | solution.py:67
  93.5 0.2 collective-permute-done.16.refs_2_
  93.7 3.9 %collective-permute-done.18.refs_5_.refs_4_.refs_1_ = bf16[256,1792]{1,0:T(8,128)(2,1)S(1)} collective-permute-done((bf16[256,1792]{1,0:T(8,128)(2,1)S(1)}, bf16[256,1792]{1,0:T(8,128)(2,1)S(1)}, u32[]{:S(2)}, u32[]{:S(2)}) %collective-permute-start.18) | collective-permute-done | bytes 917536 | tf_op jit(solution)/shard_map/ppermute | solution.py:323
  97.6 3.0 %collective-permute-done.14.refs_4_.refs_3_.refs_2_ = bf16[256,1792]{1,0:T(8,128)(2,1)S(1)} collective-permute-done((bf16[256,1792]{1,0:T(8,128)(2,1)S(1)}, bf16[256,1792]{1,0:T(8,128)(2,1)S(1)}, u32[]{:S(2)}, u32[]{:S(2)}) %collective-permute-start.14) | collective-permute-done | bytes 917536 | tf_op jit(solution)/shard_map/ppermute | solution.py:323
  100.6 0.2 shard_map.96.refs_1_
  100.9 0.3 shard_map.95.refs_0_
  101.4 3.0 %collective-permute-start.23 = (f32[8,128]{1,0:T(8,128)S(1)}, f32[8,128]{1,0:T(8,128)S(1)}, u32[]{:S(2)}, u32[]{:S(2)}) collective-permute-start(f32[8,128]{1,0:T(8,128)S(1)} %shard_map.97.refs_0_), channel_id=1, source_target_pairs={{0,17},{1,16},{16,1},{17,0},{2,19},{3,18},{18,3},{19,2},{4,21},{5,... | collective-permute-start | bytes 12296 | tf_op jit(solution)/shard_map/ppermute | solution.py:393
  104.4 1.7 %collective-permute-start.21 = (f32[8,128]{1,0:T(8,128)S(1)}, f32[8,128]{1,0:T(8,128)S(1)}, u32[]{:S(2)}, u32[]{:S(2)}) collective-permute-start(f32[8,128]{1,0:T(8,128)S(1)} %shard_map.97.refs_0_), channel_id=1, source_target_pairs={{0,1},{1,0},{16,17},{17,16},{2,3},{3,2},{18,19},{19,18},{4,5},{5,4... | collective-permute-start | bytes 12296 | tf_op jit(solution)/shard_map/ppermute | solution.py:393
  106.2 0.1 collective-permute-done.23.refs_3_
  106.3 1.7 %collective-permute-done.22.refs_2_ = f32[8,128]{1,0:T(8,128)S(1)} collective-permute-done((f32[8,128]{1,0:T(8,128)S(1)}, f32[8,128]{1,0:T(8,128)S(1)}, u32[]{:S(2)}, u32[]{:S(2)}) %collective-permute-start.22) | collective-permute-done | bytes 4128 | tf_op jit(solution)/shard_map/ppermute | solution.py:393
  108.0 1.5 %collective-permute-done.21.refs_1_ = f32[8,128]{1,0:T(8,128)S(1)} collective-permute-done((f32[8,128]{1,0:T(8,128)S(1)}, f32[8,128]{1,0:T(8,128)S(1)}, u32[]{:S(2)}, u32[]{:S(2)}) %collective-permute-start.21) | collective-permute-done | bytes 4128 | tf_op jit(solution)/shard_map/ppermute | solution.py:393
  109.5 6.0 %collective-permute-done.20.refs_2_ = bf16[256,1792]{1,0:T(8,128)(2,1)S(1)} collective-permute-done((bf16[256,1792]{1,0:T(8,128)(2,1)S(1)}, bf16[256,1792]{1,0:T(8,128)(2,1)S(1)}, u32[]{:S(2)}, u32[]{:S(2)}) %collective-permute-start.20) | collective-permute-done | bytes 917536 | tf_op jit(solution)/shard_map/ppermute | solution.py:323
  115.5 0.3 shard_map.99
  115.9 0.9 collective-permute-start.25
  116.8 0.4 shard_map.100
  117.2 3.9 %collective-permute-start.24 = (bf16[128,1792]{1,0:T(8,128)(2,1)S(1)}, bf16[128,1792]{1,0:T(8,128)(2,1)S(1)}, u32[]{:S(2)}, u32[]{:S(2)}) collective-permute-start(bf16[128,1792]{1,0:T(8,128)(2,1)S(1)} %get-tuple-element.59.refs_0_), channel_id=1, source_target_pairs={{0,1},{1,0},{2,3},{3,2},{4,5},{5,4},{6,7},{7,6},{8,9},{9,8},{10,11... | collective-permute-start | bytes 1376264 | tf_op jit(solution)/shard_map/ppermute | solution.py:328
  121.1 1.8 %collective-permute-start.28 = (f32[8,128]{1,0:T(8,128)S(1)}, f32[8,128]{1,0:T(8,128)S(1)}, u32[]{:S(2)}, u32[]{:S(2)}) collective-permute-start(f32[8,128]{1,0:T(8,128)S(1)} %shard_map.102.refs_0_), channel_id=1, source_target_pairs={{0,8},{4,12},{8,0},{12,4},{1,9},{5,13},{9,1},{13,5},{2,10},{6,14},... | collective-permute-start | bytes 12296 | tf_op jit(solution)/shard_map/ppermute | solution.py:405
  122.9 1.4 %collective-permute-start.27 = (f32[8,128]{1,0:T(8,128)S(1)}, f32[8,128]{1,0:T(8,128)S(1)}, u32[]{:S(2)}, u32[]{:S(2)}) collective-permute-start(f32[8,128]{1,0:T(8,128)S(1)} %shard_map.102.refs_0_), channel_id=1, source_target_pairs={{0,12},{4,0},{8,4},{12,8},{1,13},{5,1},{9,5},{13,9},{2,14},{6,2},{... | collective-permute-start | bytes 12296 | tf_op jit(solution)/shard_map/ppermute | solution.py:405
  124.3 0.6 collective-permute-start.26
  124.9 1.3 collective-permute-done.28.refs_3_
  126.2 0.3 collective-permute-done.27.refs_2_
  126.5 2.6 %collective-permute-done.26.refs_1_ = f32[8,128]{1,0:T(8,128)S(1)} collective-permute-done((f32[8,128]{1,0:T(8,128)S(1)}, f32[8,128]{1,0:T(8,128)S(1)}, u32[]{:S(2)}, u32[]{:S(2)}) %collective-permute-start.26) | collective-permute-done | bytes 4128 | tf_op jit(solution)/shard_map/ppermute | solution.py:405
  129.1 1.5 %collective-permute-start.30 = (f32[8,128]{1,0:T(8,128)S(1)}, f32[8,128]{1,0:T(8,128)S(1)}, u32[]{:S(2)}, u32[]{:S(2)}) collective-permute-start(f32[8,128]{1,0:T(8,128)S(1)} %shard_map.103.refs_0_), channel_id=1, source_target_pairs={{0,96},{32,0},{64,32},{96,64},{1,97},{33,1},{65,33},{97,65},{2,98}... | collective-permute-start | bytes 12296 | tf_op jit(solution)/shard_map/ppermute | solution.py:405
  130.6 0.6 collective-permute-start.29
  131.2 3.0 %collective-permute-done.31.refs_3_ = f32[8,128]{1,0:T(8,128)S(1)} collective-permute-done((f32[8,128]{1,0:T(8,128)S(1)}, f32[8,128]{1,0:T(8,128)S(1)}, u32[]{:S(2)}, u32[]{:S(2)}) %collective-permute-start.31) | collective-permute-done | bytes 4128 | tf_op jit(solution)/shard_map/ppermute | solution.py:405
  134.2 1.2 collective-permute-done.29.refs_1_
  135.4 0.5 slice.3
  136.6 1.6 %shard_map.101 = (bf16[128,1792]{1,0:T(8,128)(2,1)}, bf16[128,1792]{1,0:T(8,128)(2,1)}) custom-call(s32[1]{0:T(128)} %bitcast.pos_ref.half, bf16[256,1792]{1,0:T(8,128)(2,1)S(1)} %copy-done.1, bf16[256,1792]{1,0:T(8,128)(2,1)S(1)} %copy-done.3, f32[128,1792]{1,0:T(8,128)S(1)} %get-tuple-element.58.i_ref, ...), custom_call_target="tpu_custom_call" | custom-call | tf_op jit(solution)/shard_map/pallas_call | solution.py:67
  (41 shorter events, 0.7 us)
Async XLA Ops:
  0.6 1.2 copy-start.2
  1.8 0.7 copy-start.4
  2.7 8.9 %collective-permute-start = (bf16[128,1920]{1,0:T(8,128)(2,1)S(1)}, bf16[128,1920]{1,0:T(8,128)(2,1)S(1)}, u32[]{:S(2)}, u32[]{:S(2)}) collective-permute-start(bf16[128,1920]{1,0:T(8,128)(2,1)S(1)} %get-tuple-element.34.a_ref), channel_id=1, source_target_pairs={{0,16},{1,17},{2,19},{3,18},{16,0},{17,1},{18,3},{19,2},{4,20},{5,... | collective-permute-start | bytes 1474568 | tf_op jit(solution)/shard_map/ppermute | solution.py:337
  5.9 1.2 copy-start
  11.7 25.3 %collective-permute-start.4 = (bf16[256,1920]{1,0:T(8,128)(2,1)S(1)}, bf16[256,1920]{1,0:T(8,128)(2,1)S(1)}, u32[]{:S(2)}, u32[]{:S(2)}) collective-permute-start(bf16[256,1920]{1,0:T(8,128)(2,1)S(1)} %shard_map.78.refs_1_), channel_id=1, source_target_pairs={{0,96},{32,0},{64,32},{96,64},{1,97},{33,1},{65,33},{97,65},{2,98}... | collective-permute-start | bytes 2949128 | tf_op jit(solution)/shard_map/ppermute | solution.py:317
  15.9 24.6 %collective-permute-start.2 = (bf16[256,1920]{1,0:T(8,128)(2,1)S(1)}, bf16[256,1920]{1,0:T(8,128)(2,1)S(1)}, u32[]{:S(2)}, u32[]{:S(2)}) collective-permute-start(bf16[256,1920]{1,0:T(8,128)(2,1)S(1)} %shard_map.78.refs_1_), channel_id=1, source_target_pairs={{0,32},{32,64},{64,96},{96,0},{1,33},{33,65},{65,97},{97,1},{2,34}... | collective-permute-start | bytes 2949128 | tf_op jit(solution)/shard_map/ppermute | solution.py:317
  16.0 24.5 %collective-permute-start.7 = (bf16[256,1920]{1,0:T(8,128)(2,1)S(1)}, bf16[256,1920]{1,0:T(8,128)(2,1)S(1)}, u32[]{:S(2)}, u32[]{:S(2)}) collective-permute-start(bf16[256,1920]{1,0:T(8,128)(2,1)S(1)} %shard_map.79.refs_7_), channel_id=1, source_target_pairs={{0,12},{4,0},{8,4},{12,8},{1,13},{5,1},{9,5},{13,9},{2,14},{6,2},{... | collective-permute-start | bytes 2949128 | tf_op jit(solution)/shard_map/ppermute | solution.py:317
  18.8 24.3 %collective-permute-start.6 = (bf16[256,1920]{1,0:T(8,128)(2,1)S(1)}, bf16[256,1920]{1,0:T(8,128)(2,1)S(1)}, u32[]{:S(2)}, u32[]{:S(2)}) collective-permute-start(bf16[256,1920]{1,0:T(8,128)(2,1)S(1)} %shard_map.79.refs_7_), channel_id=1, source_target_pairs={{0,4},{4,8},{8,12},{12,0},{1,5},{5,9},{9,13},{13,1},{2,6},{6,10},{... | collective-permute-start | bytes 2949128 | tf_op jit(solution)/shard_map/ppermute | solution.py:317
  18.8 24.6 %collective-permute-start.1 = (bf16[256,1920]{1,0:T(8,128)(2,1)S(1)}, bf16[256,1920]{1,0:T(8,128)(2,1)S(1)}, u32[]{:S(2)}, u32[]{:S(2)}) collective-permute-start(bf16[256,1920]{1,0:T(8,128)(2,1)S(1)} %shard_map.78.refs_1_), channel_id=1, source_target_pairs={{0,2},{2,0},{1,3},{3,1},{4,6},{6,4},{5,7},{7,5},{8,10},{10,8},{9,1... | collective-permute-start | bytes 2949128 | tf_op jit(solution)/shard_map/ppermute | solution.py:328
  37.0 6.4 %collective-permute-start.5 = (bf16[256,1920]{1,0:T(8,128)(2,1)S(1)}, bf16[256,1920]{1,0:T(8,128)(2,1)S(1)}, u32[]{:S(2)}, u32[]{:S(2)}) collective-permute-start(bf16[256,1920]{1,0:T(8,128)(2,1)S(1)} %collective-permute-done.4.refs_5_.i_high), channel_id=1, source_target_pairs={{0,2},{2,0},{1,3},{3,1},{4,6},{6,4},{5,7},{7,5},{8,10},{10,8},{9,1... | collective-permute-start | bytes 2949128 | tf_op jit(solution)/shard_map/ppermute | solution.py:328
  40.5 3.0 %collective-permute-start.3 = (bf16[256,1920]{1,0:T(8,128)(2,1)S(1)}, bf16[256,1920]{1,0:T(8,128)(2,1)S(1)}, u32[]{:S(2)}, u32[]{:S(2)}) collective-permute-start(bf16[256,1920]{1,0:T(8,128)(2,1)S(1)} %collective-permute-done.2.refs_3_.i_low), channel_id=1, source_target_pairs={{0,2},{2,0},{1,3},{3,1},{4,6},{6,4},{5,7},{7,5},{8,10},{10,8},{9,1... | collective-permute-start | bytes 2949128 | tf_op jit(solution)/shard_map/ppermute | solution.py:328
  43.2 15.4 %collective-permute-start.8 = (bf16[256,1920]{1,0:T(8,128)(2,1)S(1)}, bf16[256,1920]{1,0:T(8,128)(2,1)S(1)}, u32[]{:S(2)}, u32[]{:S(2)}) collective-permute-start(bf16[256,1920]{1,0:T(8,128)(2,1)S(1)} %get-tuple-element.36), channel_id=1, source_target_pairs={{0,4},{2,14},{4,8},{6,2},{8,12},{10,6},{12,0},{14,10},{1,5},{3,15}... | collective-permute-start | bytes 2949128 | tf_op jit(solution)/shard_map/ppermute | solution.py:323
  43.3 15.4 %collective-permute-start.9 = (bf16[256,1920]{1,0:T(8,128)(2,1)S(1)}, bf16[256,1920]{1,0:T(8,128)(2,1)S(1)}, u32[]{:S(2)}, u32[]{:S(2)}) collective-permute-start(bf16[256,1920]{1,0:T(8,128)(2,1)S(1)} %get-tuple-element.41), channel_id=1, source_target_pairs={{0,32},{2,98},{32,64},{34,2},{64,96},{66,34},{96,0},{98,66},{1,33}... | collective-permute-start | bytes 2949128 | tf_op jit(solution)/shard_map/ppermute | solution.py:323
  58.8 3.8 %collective-permute-start.10 = (bf16[256,1920]{1,0:T(8,128)(2,1)S(1)}, bf16[256,1920]{1,0:T(8,128)(2,1)S(1)}, u32[]{:S(2)}, u32[]{:S(2)}) collective-permute-start(bf16[256,1920]{1,0:T(8,128)(2,1)S(1)} %shard_map.83.refs_1_), channel_id=1, source_target_pairs={{0,2},{2,0},{1,3},{3,1},{4,6},{6,4},{5,7},{7,5},{8,10},{10,8},{9,1... | collective-permute-start | bytes 2949128 | tf_op jit(solution)/shard_map/ppermute | solution.py:328
  69.2 5.3 %collective-permute-start.12 = (bf16[272,1792]{1,0:T(8,128)(2,1)S(1)}, bf16[272,1792]{1,0:T(8,128)(2,1)S(1)}, u32[]{:S(2)}, u32[]{:S(2)}) collective-permute-start(bf16[272,1792]{1,0:T(8,128)(2,1)S(1)} %get-tuple-element.50), channel_id=1, source_target_pairs={{0,2},{2,0},{1,3},{3,1},{4,6},{6,4},{5,7},{7,5},{8,10},{10,8},{9,1... | collective-permute-start | bytes 2924552 | tf_op jit(solution)/shard_map/ppermute | solution.py:328
  71.9 3.5 %collective-permute-start.11 = (bf16[256,1792]{1,0:T(8,128)(2,1)S(1)}, bf16[256,1792]{1,0:T(8,128)(2,1)S(1)}, u32[]{:S(2)}, u32[]{:S(2)}) collective-permute-start(bf16[256,1792]{1,0:T(8,128)(2,1)S(1)} %get-tuple-element.49), channel_id=1, source_target_pairs={{0,2},{2,0},{1,3},{3,1},{4,6},{6,4},{5,7},{7,5},{8,10},{10,8},{9,1... | collective-permute-start | bytes 2752520 | tf_op jit(solution)/shard_map/ppermute | solution.py:328
  74.1 17.2 %collective-permute-start.17 = (bf16[256,1792]{1,0:T(8,128)(2,1)S(1)}, bf16[256,1792]{1,0:T(8,128)(2,1)S(1)}, u32[]{:S(2)}, u32[]{:S(2)}) collective-permute-start(bf16[256,1792]{1,0:T(8,128)(2,1)S(1)} %shard_map.87.refs_3_), channel_id=1, source_target_pairs={{0,4},{2,14},{4,8},{6,2},{8,12},{10,6},{12,0},{14,10},{1,5},{3,15}... | collective-permute-start | bytes 2752520 | tf_op jit(solution)/shard_map/ppermute | solution.py:323
  75.0 18.7 %collective-permute-start.16 = (bf16[256,1792]{1,0:T(8,128)(2,1)S(1)}, bf16[256,1792]{1,0:T(8,128)(2,1)S(1)}, u32[]{:S(2)}, u32[]{:S(2)}) collective-permute-start(bf16[256,1792]{1,0:T(8,128)(2,1)S(1)} %get-tuple-element.51.refs_2_), channel_id=1, source_target_pairs={{0,32},{2,98},{32,64},{34,2},{64,96},{66,34},{96,0},{98,66},{1,33}... | collective-permute-start | bytes 2752520 | tf_op jit(solution)/shard_map/ppermute | solution.py:323
  77.7 22.9 %collective-permute-start.14 = (bf16[256,1792]{1,0:T(8,128)(2,1)S(1)}, bf16[256,1792]{1,0:T(8,128)(2,1)S(1)}, u32[]{:S(2)}, u32[]{:S(2)}) collective-permute-start(bf16[256,1792]{1,0:T(8,128)(2,1)S(1)} %shard_map.89.refs_4_), channel_id=1, source_target_pairs={{0,96},{2,34},{32,0},{34,66},{64,32},{66,98},{96,64},{98,2},{1,97}... | collective-permute-start | bytes 2752520 | tf_op jit(solution)/shard_map/ppermute | solution.py:323
  81.0 16.6 %collective-permute-start.18 = (bf16[256,1792]{1,0:T(8,128)(2,1)S(1)}, bf16[256,1792]{1,0:T(8,128)(2,1)S(1)}, u32[]{:S(2)}, u32[]{:S(2)}) collective-permute-start(bf16[256,1792]{1,0:T(8,128)(2,1)S(1)} %shard_map.90.refs_4_), channel_id=1, source_target_pairs={{0,12},{2,6},{4,0},{6,10},{8,4},{10,14},{12,8},{14,2},{1,13},{3,7}... | collective-permute-start | bytes 2752520 | tf_op jit(solution)/shard_map/ppermute | solution.py:323
  90.3 10.6 %collective-permute-start.13 = (bf16[256,1792]{1,0:T(8,128)(2,1)S(1)}, bf16[256,1792]{1,0:T(8,128)(2,1)S(1)}, u32[]{:S(2)}, u32[]{:S(2)}) collective-permute-start(bf16[256,1792]{1,0:T(8,128)(2,1)S(1)} %get-tuple-element.54), channel_id=1, source_target_pairs={{0,2},{2,0},{1,3},{3,1},{4,6},{6,4},{5,7},{7,5},{8,10},{10,8},{9,1... | collective-permute-start | bytes 2752520 | tf_op jit(solution)/shard_map/ppermute | solution.py:328
  91.4 9.6 %collective-permute-start.15 = (bf16[256,1792]{1,0:T(8,128)(2,1)S(1)}, bf16[256,1792]{1,0:T(8,128)(2,1)S(1)}, u32[]{:S(2)}, u32[]{:S(2)}) collective-permute-start(bf16[256,1792]{1,0:T(8,128)(2,1)S(1)} %get-tuple-element.55), channel_id=1, source_target_pairs={{0,2},{2,0},{1,3},{3,1},{4,6},{6,4},{5,7},{7,5},{8,10},{10,8},{9,1... | collective-permute-start | bytes 2752520 | tf_op jit(solution)/shard_map/ppermute | solution.py:328
  100.8 14.7 %collective-permute-start.20 = (bf16[256,1792]{1,0:T(8,128)(2,1)S(1)}, bf16[256,1792]{1,0:T(8,128)(2,1)S(1)}, u32[]{:S(2)}, u32[]{:S(2)}) collective-permute-start(bf16[256,1792]{1,0:T(8,128)(2,1)S(1)} %shard_map.96.refs_1_), channel_id=1, source_target_pairs={{0,4},{2,14},{4,8},{6,2},{8,12},{10,6},{12,0},{14,10},{1,5},{3,15}... | collective-permute-start | bytes 2752520 | tf_op jit(solution)/shard_map/ppermute | solution.py:323
  101.3 15.5 %collective-permute-start.19 = (bf16[256,1792]{1,0:T(8,128)(2,1)S(1)}, bf16[256,1792]{1,0:T(8,128)(2,1)S(1)}, u32[]{:S(2)}, u32[]{:S(2)}) collective-permute-start(bf16[256,1792]{1,0:T(8,128)(2,1)S(1)} %shard_map.95.refs_0_), channel_id=1, source_target_pairs={{0,32},{2,98},{32,64},{34,2},{64,96},{66,34},{96,0},{98,66},{1,33}... | collective-permute-start | bytes 2752520 | tf_op jit(solution)/shard_map/ppermute | solution.py:323
  101.4 4.9 %collective-permute-start.23 = (f32[8,128]{1,0:T(8,128)S(1)}, f32[8,128]{1,0:T(8,128)S(1)}, u32[]{:S(2)}, u32[]{:S(2)}) collective-permute-start(f32[8,128]{1,0:T(8,128)S(1)} %shard_map.97.refs_0_), channel_id=1, source_target_pairs={{0,17},{1,16},{16,1},{17,0},{2,19},{3,18},{18,3},{19,2},{4,21},{5,... | collective-permute-start | bytes 12296 | tf_op jit(solution)/shard_map/ppermute | solution.py:393
  104.4 3.6 %collective-permute-start.22 = (f32[8,128]{1,0:T(8,128)S(1)}, f32[8,128]{1,0:T(8,128)S(1)}, u32[]{:S(2)}, u32[]{:S(2)}) collective-permute-start(f32[8,128]{1,0:T(8,128)S(1)} %shard_map.97.refs_0_), channel_id=1, source_target_pairs={{0,16},{1,17},{16,0},{17,1},{2,18},{3,19},{18,2},{19,3},{4,20},{5,... | collective-permute-start | bytes 12296 | tf_op jit(solution)/shard_map/ppermute | solution.py:393
  104.4 5.1 %collective-permute-start.21 = (f32[8,128]{1,0:T(8,128)S(1)}, f32[8,128]{1,0:T(8,128)S(1)}, u32[]{:S(2)}, u32[]{:S(2)}) collective-permute-start(f32[8,128]{1,0:T(8,128)S(1)} %shard_map.97.refs_0_), channel_id=1, source_target_pairs={{0,1},{1,0},{16,17},{17,16},{2,3},{3,2},{18,19},{19,18},{4,5},{5,4... | collective-permute-start | bytes 12296 | tf_op jit(solution)/shard_map/ppermute | solution.py:393
  115.8 20.8 %copy-start.1 = (bf16[256,1792]{1,0:T(8,128)(2,1)S(1)}, bf16[256,1792]{1,0:T(8,128)(2,1)}, u32[]{:S(2)}) copy-start(bf16[256,1792]{1,0:T(8,128)(2,1)} %img_ref.3) | copy-start | bytes 2752516
  115.8 20.8 %copy-start.3 = (bf16[256,1792]{1,0:T(8,128)(2,1)S(1)}, bf16[256,1792]{1,0:T(8,128)(2,1)}, u32[]{:S(2)}) copy-start(bf16[256,1792]{1,0:T(8,128)(2,1)} %txt_ref.3) | copy-start | bytes 2752516
  115.9 20.7 %collective-permute-start.25 = (bf16[128,1792]{1,0:T(8,128)(2,1)S(1)}, bf16[128,1792]{1,0:T(8,128)(2,1)S(1)}, u32[]{:S(2)}, u32[]{:S(2)}) collective-permute-start(bf16[128,1792]{1,0:T(8,128)(2,1)S(1)} %get-tuple-element.57.refs_4_), channel_id=1, source_target_pairs={{0,16},{1,17},{2,19},{3,18},{16,0},{17,1},{18,3},{19,2},{4,20},{5,... | collective-permute-start | bytes 1376264 | tf_op jit(solution)/shard_map/ppermute | solution.py:337
  117.2 19.3 %collective-permute-start.24 = (bf16[128,1792]{1,0:T(8,128)(2,1)S(1)}, bf16[128,1792]{1,0:T(8,128)(2,1)S(1)}, u32[]{:S(2)}, u32[]{:S(2)}) collective-permute-start(bf16[128,1792]{1,0:T(8,128)(2,1)S(1)} %get-tuple-element.59.refs_0_), channel_id=1, source_target_pairs={{0,1},{1,0},{2,3},{3,2},{4,5},{5,4},{6,7},{7,6},{8,9},{9,8},{10,11... | collective-permute-start | bytes 1376264 | tf_op jit(solution)/shard_map/ppermute | solution.py:328
  121.1 5.1 %collective-permute-start.28 = (f32[8,128]{1,0:T(8,128)S(1)}, f32[8,128]{1,0:T(8,128)S(1)}, u32[]{:S(2)}, u32[]{:S(2)}) collective-permute-start(f32[8,128]{1,0:T(8,128)S(1)} %shard_map.102.refs_0_), channel_id=1, source_target_pairs={{0,8},{4,12},{8,0},{12,4},{1,9},{5,13},{9,1},{13,5},{2,10},{6,14},... | collective-permute-start | bytes 12296 | tf_op jit(solution)/shard_map/ppermute | solution.py:405
  122.9 3.6 %collective-permute-start.27 = (f32[8,128]{1,0:T(8,128)S(1)}, f32[8,128]{1,0:T(8,128)S(1)}, u32[]{:S(2)}, u32[]{:S(2)}) collective-permute-start(f32[8,128]{1,0:T(8,128)S(1)} %shard_map.102.refs_0_), channel_id=1, source_target_pairs={{0,12},{4,0},{8,4},{12,8},{1,13},{5,1},{9,5},{13,9},{2,14},{6,2},{... | collective-permute-start | bytes 12296 | tf_op jit(solution)/shard_map/ppermute | solution.py:405
  124.3 4.8 %collective-permute-start.26 = (f32[8,128]{1,0:T(8,128)S(1)}, f32[8,128]{1,0:T(8,128)S(1)}, u32[]{:S(2)}, u32[]{:S(2)}) collective-permute-start(f32[8,128]{1,0:T(8,128)S(1)} %shard_map.102.refs_0_), channel_id=1, source_target_pairs={{0,4},{4,8},{8,12},{12,0},{1,5},{5,9},{9,13},{13,1},{2,6},{6,10},{... | collective-permute-start | bytes 12296 | tf_op jit(solution)/shard_map/ppermute | solution.py:405
  129.1 5.1 %collective-permute-start.31 = (f32[8,128]{1,0:T(8,128)S(1)}, f32[8,128]{1,0:T(8,128)S(1)}, u32[]{:S(2)}, u32[]{:S(2)}) collective-permute-start(f32[8,128]{1,0:T(8,128)S(1)} %shard_map.103.refs_0_), channel_id=1, source_target_pairs={{0,64},{32,96},{64,0},{96,32},{1,65},{33,97},{65,1},{97,33},{2,66}... | collective-permute-start | bytes 12296 | tf_op jit(solution)/shard_map/ppermute | solution.py:405
  129.1 5.1 %collective-permute-start.30 = (f32[8,128]{1,0:T(8,128)S(1)}, f32[8,128]{1,0:T(8,128)S(1)}, u32[]{:S(2)}, u32[]{:S(2)}) collective-permute-start(f32[8,128]{1,0:T(8,128)S(1)} %shard_map.103.refs_0_), channel_id=1, source_target_pairs={{0,96},{32,0},{64,32},{96,64},{1,97},{33,1},{65,33},{97,65},{2,98}... | collective-permute-start | bytes 12296 | tf_op jit(solution)/shard_map/ppermute | solution.py:405
  130.6 4.8 %collective-permute-start.29 = (f32[8,128]{1,0:T(8,128)S(1)}, f32[8,128]{1,0:T(8,128)S(1)}, u32[]{:S(2)}, u32[]{:S(2)}) collective-permute-start(f32[8,128]{1,0:T(8,128)S(1)} %shard_map.103.refs_0_), channel_id=1, source_target_pairs={{0,32},{32,64},{64,96},{96,0},{1,33},{33,65},{65,97},{97,1},{2,34}... | collective-permute-start | bytes 12296 | tf_op jit(solution)/shard_map/ppermute | solution.py:405
